TPU v7x, 32 devices: a whole 2x2x4 slice. The times are simulated.
32 devices in a mesh: dp: 8 (over z, x), mp: 4 (over y, core).
Axes of the slice: x: 2, y: 2, z: 4, core: 2. Of those that a mesh axis runs over, the one named last changes fastest.
Arguments:
- latents: float32 [16, 64, 1536], P('dp', 'mp'), may hold values from -6 to 6
- media: bfloat16 [16, 2048, 1536], P('dp', 'mp'), may hold values from -6 to 6
- frames: int32 [16], P('dp'), may hold values from 1 to 8, as said below
- cotangent: float32 [16, 64, 1536], P('dp', 'mp'), may hold values from -16 to 16
- qkv_master: float32 [3, 1536, 1536], P(None, 'dp', 'mp'), may hold values from -0.15625 to 0.15625
- qkv_momentum: float32 [3, 1536, 1536], P(None, 'dp', 'mp'), may hold values from -0.001953125 to 0.001953125
- qkv_average: float32 [3, 1536, 1536], P(None, 'dp', 'mp'), may hold values from -0.15625 to 0.15625
- out_master: float32 [1536, 1536], P('mp', 'dp'), may hold values from -8 to 8
- out_momentum: float32 [1536, 1536], P('mp', 'dp'), may hold values from -0.00024414062 to 0.00024414062
- out_average: float32 [1536, 1536], P('mp', 'dp'), may hold values from -0.75 to 0.75
- up_master: float32 [1536, 6144], P('dp', 'mp'), may hold values from -2 to 2
- up_momentum: float32 [1536, 6144], P('dp', 'mp'), may hold values from -0.00048828125 to 0.00048828125
- up_average: float32 [1536, 6144], P('dp', 'mp'), may hold values from -0.15625 to 0.15625
- down_master: float32 [6144, 1536], P('mp', 'dp'), may hold values from -2 to 2
- down_momentum: float32 [6144, 1536], P('mp', 'dp'), may hold values from -0.0008544922 to 0.0008544922
- down_average: float32 [6144, 1536], P('mp', 'dp'), may hold values from -0.078125 to 0.078125
- norm_params: float32 [6, 1536], replicated, may hold values from -2 to 4
- norm_momentum: float32 [6, 1536], replicated, may hold values from -0.0017089844 to 0.0017089844
- norm_average: float32 [6, 1536], replicated, may hold values from 0.5 to 1.5
- time_table: float32 [8, 1536], replicated, may hold values from -3 to 3
- time_momentum: float32 [8, 1536], replicated, may hold values from -0.0007324219 to 0.0007324219
- time_average: float32 [8, 1536], replicated, may hold values from -3 to 3
Outputs:
- latents_out: float32 [16, 64, 1536], P('dp', 'mp')
- latents_grad: float32 [16, 64, 1536], P('dp', 'mp')
- media_grad: float32 [16, 2048, 1536], P('dp', 'mp')
- grad_norm: float32 [], replicated
- qkv_grad: float32 [3, 1536, 1536], P(None, 'dp', 'mp')
- qkv_new: float32 [3, 1536, 1536], P(None, 'dp', 'mp')
- qkv_momentum_new: float32 [3, 1536, 1536], P(None, 'dp', 'mp')
- qkv_average_new: float32 [3, 1536, 1536], P(None, 'dp', 'mp')
- out_grad: float32 [1536, 1536], P('mp', 'dp')
- out_new: float32 [1536, 1536], P('mp', 'dp')
- out_momentum_new: float32 [1536, 1536], P('mp', 'dp')
- out_average_new: float32 [1536, 1536], P('mp', 'dp')
- up_grad: float32 [1536, 6144], P('dp', 'mp')
- up_new: float32 [1536, 6144], P('dp', 'mp')
- up_momentum_new: float32 [1536, 6144], P('dp', 'mp')
- up_average_new: float32 [1536, 6144], P('dp', 'mp')
- down_grad: float32 [6144, 1536], P('mp', 'dp')
- down_new: float32 [6144, 1536], P('mp', 'dp')
- down_momentum_new: float32 [6144, 1536], P('mp', 'dp')
- down_average_new: float32 [6144, 1536], P('mp', 'dp')
- norm_grad: float32 [6, 1536], replicated
- norm_new: float32 [6, 1536], replicated
- norm_momentum_new: float32 [6, 1536], replicated
- norm_average_new: float32 [6, 1536], replicated
- time_grad: float32 [8, 1536], replicated
- time_new: float32 [8, 1536], replicated
- time_momentum_new: float32 [8, 1536], replicated
- time_average_new: float32 [8, 1536], replicated
- qkv_copy: bfloat16 [3, 1536, 1536], P(None, 'dp', 'mp')
- out_copy: bfloat16 [1536, 1536], P('mp', 'dp')
- up_copy: bfloat16 [1536, 6144], P('dp', 'mp')
- down_copy: bfloat16 [6144, 1536], P('mp', 'dp')
Inputs may be any that keep to these rules, and one draw needn't show every extreme that they name: Every item has 1 or 8 frames, and among the 2 items of each index of dp at least one has 8.
All inputs are finite; a program needn't handle non-finite values.
Results may differ from a plain program's by a relative error of at most 0.018.
The roundings to bfloat16 on the way count: a program that leaves them out, or rounds other values in their place, can miss the bound.
Values may be sent and summed in bfloat16 or wider, within the bound.
A program may use at most 192 MiB of HBM per device.

v0:
```python
import jax
import jax.numpy as jnp
from jax import lax
from jax.sharding import PartitionSpec as P

HEAD_DIM = 96
FRAMES = 8
PATCHES = 256


EPS = 1e-05
MOMENT = 0.9
STEP_RATES = (30.0, 1200.0, 120.0, 40.0, 1000.0, 1200.0)
DECAY_AVG = 0.75
HIGH = lax.Precision.HIGHEST
NEGATIVE = -1e30


def layer_norm(values, factor, offset):
    centered = values - jnp.mean(values, axis=-1, keepdims=True)
    variance = jnp.mean(centered * centered, axis=-1, keepdims=True)
    return centered * lax.rsqrt(variance + EPS) * factor + offset


def exact_gelu(values):
    return jax.nn.gelu(values, approximate=False)


def square_sum(arrays):
    running = jnp.zeros((), jnp.float32)
    for member in arrays:
        running = running + jnp.sum(member * member)
    return running


def advance(gradient, master, momentum, average, clip_factor, rate):
    clipped = gradient * clip_factor
    moment_new = MOMENT * momentum + clipped
    master_new = master - rate * (clipped + MOMENT * moment_new)
    average_new = DECAY_AVG * average + (1.0 - DECAY_AVG) * master_new
    return (clipped, master_new, moment_new, average_new)


def shards(
    latents,
    media,
    frames,
    cotangent,
    qkv_master,
    qkv_momentum,
    qkv_average,
    out_master,
    out_momentum,
    out_average,
    up_master,
    up_momentum,
    up_average,
    down_master,
    down_momentum,
    down_average,
    norm_params,
    norm_momentum,
    norm_average,
    time_table,
    time_momentum,
    time_average,
):
    f32 = jnp.float32
    half = jnp.bfloat16
    mp_rank = lax.axis_index("mp")
    mp_count = lax.axis_size("mp")
    item_count = latents.shape[0]
    local_slots = media.shape[1]
    all_slots = local_slots * mp_count
    scale_factor = HEAD_DIM ** (-0.5)
    qkv_weight, out_weight, up_weight, down_weight = (
        lax.all_gather(qkv_master.astype(half), "dp", axis=1, tiled=True),
        lax.all_gather(out_master.astype(half), "dp", axis=1, tiled=True),
        lax.all_gather(up_master.astype(half), "dp", axis=0, tiled=True),
        lax.all_gather(down_master.astype(half), "dp", axis=1, tiled=True),
    )
    w_query = qkv_weight[0]
    w_keyval = jnp.concatenate([qkv_weight[1], qkv_weight[2]], axis=1)
    local_width = w_query.shape[1]
    head_count = local_width // HEAD_DIM
    slot_ids = mp_rank * local_slots + jnp.arange(local_slots)
    frame_ids = slot_ids // PATCHES
    onehot = (frame_ids[:, None] == jnp.arange(FRAMES)[None, :]).astype(f32)
    media_in = media.astype(f32) + jnp.dot(onehot, time_table, precision=HIGH)[None]
    media_norm = layer_norm(media_in, norm_params[0], norm_params[1]).astype(half)
    latent_norm = layer_norm(latents, norm_params[2], norm_params[3]).astype(half)
    media_rows, latent_rows = (
        lax.all_gather(media_norm, "mp", axis=1, tiled=True),
        lax.all_gather(latent_norm, "mp", axis=1, tiled=True),
    )
    lat_total = latent_rows.shape[1]
    queries = jnp.einsum("ild,de->ile", latent_rows, w_query, preferred_element_type=f32).astype(
        half
    )
    kv_media = jnp.einsum("icd,de->ice", media_rows, w_keyval, preferred_element_type=f32)
    kv_latent = jnp.einsum("ild,de->ile", latent_rows, w_keyval, preferred_element_type=f32)
    keyval = jnp.concatenate([kv_media, kv_latent], axis=1).astype(half)
    key_count = keyval.shape[1]
    keys_h = keyval[..., :local_width].reshape(item_count, key_count, head_count, HEAD_DIM)
    values_h = keyval[..., local_width:].reshape(item_count, key_count, head_count, HEAD_DIM)
    queries_h = queries.reshape(item_count, lat_total, head_count, HEAD_DIM)
    raw_scores = jnp.einsum("iqhd,ikhd->ihqk", queries_h, keys_h, preferred_element_type=f32)
    all_frames = jnp.arange(all_slots) // PATCHES
    keep_mask = jnp.concatenate(
        [all_frames[None, :] < frames[:, None], jnp.ones((item_count, lat_total), jnp.bool_)],
        axis=1,
    )
    scores = jnp.where(keep_mask[:, None, None, :], raw_scores * scale_factor, NEGATIVE)
    attention = jax.nn.softmax(scores, axis=-1)
    prob_low = attention.astype(half)
    mixed_heads = jnp.einsum("ihqk,ikhd->iqhd", prob_low, values_h, preferred_element_type=f32)
    mixed_heads = mixed_heads.reshape(item_count, lat_total, local_width).astype(half)
    attn_part = jnp.einsum("ile,ed->ild", mixed_heads, out_weight, preferred_element_type=f32)
    after_attn = latents + lax.psum_scatter(attn_part, "mp", scatter_dimension=1, tiled=True)
    ffn_norm = layer_norm(after_attn, norm_params[4], norm_params[5]).astype(half)
    ffn_rows = lax.all_gather(ffn_norm, "mp", axis=1, tiled=True)
    pre_act = jnp.einsum("ild,df->ilf", ffn_rows, up_weight, preferred_element_type=f32)
    hidden = exact_gelu(pre_act).astype(half)
    ffn_part = jnp.einsum("ilf,fd->ild", hidden, down_weight, preferred_element_type=f32)
    latents_out = after_attn + lax.psum_scatter(
        ffn_part.astype(jnp.bfloat16), "mp", scatter_dimension=1, tiled=True
    ).astype(jnp.float32)
    back_rows = lax.all_gather(cotangent.astype(half), "mp", axis=1, tiled=True)
    down_part = jnp.einsum("ilf,ild->fd", hidden, back_rows, preferred_element_type=f32)
    hidden_back = jnp.einsum("ild,fd->ilf", back_rows, down_weight, preferred_element_type=f32)
    gelu_pull = jax.vjp(exact_gelu, pre_act)[1]
    pre_back = gelu_pull(hidden_back)[0].astype(half)
    up_part = jnp.einsum("ild,ilf->df", ffn_rows, pre_back, preferred_element_type=f32)
    ffn_norm_part = jnp.einsum("ilf,df->ild", pre_back, up_weight, preferred_element_type=f32)
    ffn_norm_back = lax.psum_scatter(ffn_norm_part, "mp", scatter_dimension=1, tiled=True)
    ffn_pull = jax.vjp(layer_norm, after_attn, norm_params[4], norm_params[5])[1]
    through_ffn, ffn_factor_grad, ffn_offset_grad = ffn_pull(ffn_norm_back)
    after_back = cotangent + through_ffn
    attn_rows = lax.all_gather(after_back.astype(half), "mp", axis=1, tiled=True)
    out_part = jnp.einsum("ile,ild->ed", mixed_heads, attn_rows, preferred_element_type=f32)
    mixed_back = jnp.einsum(
        "ild,ed->ile", attn_rows, out_weight, preferred_element_type=f32
    ).astype(half)
    mixed_back = mixed_back.reshape(item_count, lat_total, head_count, HEAD_DIM)
    prob_back = jnp.einsum("iqhd,ikhd->ihqk", mixed_back, values_h, preferred_element_type=f32)
    row_terms = jnp.sum(attention * prob_back, axis=-1, keepdims=True)
    score_back = (attention * (prob_back - row_terms) * scale_factor).astype(half)
    query_back = jnp.einsum(
        "ihqk,ikhd->iqhd", score_back, keys_h, preferred_element_type=f32
    ).astype(half)
    query_back = query_back.reshape(item_count, lat_total, local_width)
    key_back = jnp.einsum(
        "ihqk,iqhd->ikhd", score_back, queries_h, preferred_element_type=f32
    ).astype(half)
    value_back = jnp.einsum(
        "ihqk,iqhd->ikhd", prob_low, mixed_back, preferred_element_type=f32
    ).astype(half)
    keyval_back = jnp.concatenate(
        [
            key_back.reshape(item_count, key_count, local_width),
            value_back.reshape(item_count, key_count, local_width),
        ],
        axis=2,
    )
    media_kv_back = keyval_back[:, :all_slots]
    latent_kv_back = keyval_back[:, all_slots:]
    query_grad = jnp.einsum("ild,ile->de", latent_rows, query_back, preferred_element_type=f32)
    keyval_grad = jnp.einsum(
        "icd,ice->de", media_rows, media_kv_back, preferred_element_type=f32
    ) + jnp.einsum("ild,ile->de", latent_rows, latent_kv_back, preferred_element_type=f32)
    qkv_part = jnp.stack([query_grad, keyval_grad[:, :local_width], keyval_grad[:, local_width:]])
    latent_norm_part = jnp.einsum(
        "ile,de->ild", query_back, w_query, preferred_element_type=f32
    ) + jnp.einsum("ile,de->ild", latent_kv_back, w_keyval, preferred_element_type=f32)
    media_norm_part = jnp.einsum("ice,de->icd", media_kv_back, w_keyval, preferred_element_type=f32)
    media_norm_back, latent_norm_back = (
        lax.psum_scatter(
            media_norm_part.astype(jnp.bfloat16), "mp", scatter_dimension=1, tiled=True
        ).astype(jnp.float32),
        lax.psum_scatter(
            latent_norm_part.astype(jnp.bfloat16), "mp", scatter_dimension=1, tiled=True
        ).astype(jnp.float32),
    )
    media_pull = jax.vjp(layer_norm, media_in, norm_params[0], norm_params[1])[1]
    media_grad, media_factor_grad, media_offset_grad = media_pull(media_norm_back)
    latent_pull = jax.vjp(layer_norm, latents, norm_params[2], norm_params[3])[1]
    through_latent, latent_factor_grad, latent_offset_grad = latent_pull(latent_norm_back)
    latents_grad = after_back + through_latent
    time_part = jnp.dot(onehot.T, jnp.sum(media_grad, axis=0), precision=HIGH)
    norm_part = jnp.stack(
        [
            media_factor_grad,
            media_offset_grad,
            latent_factor_grad,
            latent_offset_grad,
            ffn_factor_grad,
            ffn_offset_grad,
        ]
    )
    summed = (
        lax.psum(qkv_part.astype(jnp.bfloat16), "dp").astype(jnp.float32),
        lax.psum(out_part.astype(jnp.bfloat16), "dp").astype(jnp.float32),
        lax.psum(up_part.astype(jnp.bfloat16), "dp").astype(jnp.float32),
        lax.psum(down_part.astype(jnp.bfloat16), "dp").astype(jnp.float32),
    )
    small_norm, small_time = lax.psum((norm_part, time_part), ("dp", "mp"))
    big_square = lax.psum(square_sum(summed), "mp")
    dp_rank = lax.axis_index("dp")
    dp_count = lax.axis_size("dp")

    def own_piece(whole_array, axis_dim):
        piece_len = whole_array.shape[axis_dim] // dp_count
        return lax.dynamic_slice_in_dim(whole_array, dp_rank * piece_len, piece_len, axis_dim)

    owned_grads = (
        own_piece(summed[0], 1),
        own_piece(summed[1], 1),
        own_piece(summed[2], 0),
        own_piece(summed[3], 1),
    )
    grad_norm = jnp.sqrt(big_square + square_sum((small_norm, small_time)))
    clip_factor = 1.0 / jnp.maximum(grad_norm, 1.0)
    qkv_grad, qkv_new, qkv_momentum_new, qkv_average_new = advance(
        owned_grads[0], qkv_master, qkv_momentum, qkv_average, clip_factor, STEP_RATES[0]
    )
    out_grad, out_new, out_momentum_new, out_average_new = advance(
        owned_grads[1], out_master, out_momentum, out_average, clip_factor, STEP_RATES[1]
    )
    up_grad, up_new, up_momentum_new, up_average_new = advance(
        owned_grads[2], up_master, up_momentum, up_average, clip_factor, STEP_RATES[2]
    )
    down_grad, down_new, down_momentum_new, down_average_new = advance(
        owned_grads[3], down_master, down_momentum, down_average, clip_factor, STEP_RATES[3]
    )
    norm_grad, norm_new, norm_momentum_new, norm_average_new = advance(
        small_norm, norm_params, norm_momentum, norm_average, clip_factor, STEP_RATES[4]
    )
    time_grad, time_new, time_momentum_new, time_average_new = advance(
        small_time, time_table, time_momentum, time_average, clip_factor, STEP_RATES[5]
    )
    return (
        latents_out,
        latents_grad,
        media_grad,
        grad_norm,
        qkv_grad,
        qkv_new,
        qkv_momentum_new,
        qkv_average_new,
        out_grad,
        out_new,
        out_momentum_new,
        out_average_new,
        up_grad,
        up_new,
        up_momentum_new,
        up_average_new,
        down_grad,
        down_new,
        down_momentum_new,
        down_average_new,
        norm_grad,
        norm_new,
        norm_momentum_new,
        norm_average_new,
        time_grad,
        time_new,
        time_momentum_new,
        time_average_new,
        qkv_new.astype(half),
        out_new.astype(half),
        up_new.astype(half),
        down_new.astype(half),
    )


def solution(mesh):
    placed = (
        P("dp", "mp", None),
        P("dp", "mp", None),
        P("dp"),
        P("dp", "mp", None),
        P(None, "dp", "mp"),
        P(None, "dp", "mp"),
        P(None, "dp", "mp"),
        P("mp", "dp"),
        P("mp", "dp"),
        P("mp", "dp"),
        P("dp", "mp"),
        P("dp", "mp"),
        P("dp", "mp"),
        P("mp", "dp"),
        P("mp", "dp"),
        P("mp", "dp"),
        P(),
        P(),
        P(),
        P(),
        P(),
        P(),
    )
    return jax.shard_map(
        shards,
        mesh=mesh,
        in_specs=placed,
        out_specs=(
            P("dp", "mp", None),
            P("dp", "mp", None),
            P("dp", "mp", None),
            P(),
            P(None, "dp", "mp"),
            P(None, "dp", "mp"),
            P(None, "dp", "mp"),
            P(None, "dp", "mp"),
            P("mp", "dp"),
            P("mp", "dp"),
            P("mp", "dp"),
            P("mp", "dp"),
            P("dp", "mp"),
            P("dp", "mp"),
            P("dp", "mp"),
            P("dp", "mp"),
            P("mp", "dp"),
            P("mp", "dp"),
            P("mp", "dp"),
            P("mp", "dp"),
            P(),
            P(),
            P(),
            P(),
            P(),
            P(),
            P(),
            P(),
            P(None, "dp", "mp"),
            P("mp", "dp"),
            P("dp", "mp"),
            P("mp", "dp"),
        ),
        check_vma=False,
    )
```

profile of v0, /device:TPU:0, one launch (start us, length us, event | category | flops | bytes accessed | tf_op | source)
XLA Modules:
  0.0 1270.6 jit_solution(3954282026445374189)
XLA Ops:
  20.1 8.1 all_gather.29
  29.0 49.8 %all-gather.8.cloned.1.call-done = bf16[3,1536,384]{2,1,0:T(8,128)(2,1)} async-done(((bf16[3,192,384]{2,1,0:T(8,128)(2,1)}), bf16[3,1536,384]{2,1,0:T(8,128)(2,1)}) %all-gather.8.cloned.1.call-update) | async-done | bytes 3538960 | tf_op jit(solution)/shard_map/all_gather | solution.py:77
  83.6 77.9 %all-gather.6.cloned.1.call-done = bf16[2,2048,1536]{2,1,0:T(8,128)(2,1)} async-done(((bf16[2,512,1536]{2,1,0:T(8,128)(2,1)}), bf16[2,2048,1536]{2,1,0:T(8,128)(2,1)}) %all-gather.6.cloned.1.call-update) | async-done | bytes 12582928 | tf_op jit(solution)/shard_map/all_gather | solution.py:93
  161.5 12.9 %convolution_convert_fusion.3 = bf16[2,2048,768]{2,1,0:T(8,128)(2,1)S(1)} fusion(bf16[2,2048,1536]{2,1,0:T(8,128)(2,1)} %all-gather.6.cloned.1.call-done, bf16[1536,384]{1,0:T(8,128)(2,1)S(1)} %get-tuple-element.152, bf16[1536,384]{1,0:T(8,128)(2,1)S(1)} %get-tuple-element.151), kind=kOutput, calls=%fused_computation.44 | convolution fusion | flops 9671540736 | bytes 21233664 | tf_op jit(solution)/shard_map/icd,de->ice/dot_general | solution.py:100
  181.9 5.4 copy.82
  187.3 6.2 fusion.114
  199.6 5.7 all-gather.10.cloned.1.call-done
  213.5 6.9 all_gather.34
  220.4 10.0 reduce-scatter.6.cloned.1.call-done
  232.3 6.8 all_gather.31
  239.1 74.0 %all-gather.12.cloned.1.call-done = bf16[1536,1536]{1,0:T(8,128)(2,1)} async-done(((bf16[192,1536]{1,0:T(8,128)(2,1)}), bf16[1536,1536]{1,0:T(8,128)(2,1)}) %all-gather.12.cloned.1.call-update) | async-done | bytes 4718608 | tf_op jit(solution)/shard_map/all_gather | solution.py:79
  313.1 5.1 fusion.74
  318.2 75.8 %all-gather.14.cloned.1.call-done = bf16[1536,1536]{0,1:T(8,128)(2,1)} async-done(((bf16[1536,192]{0,1:T(8,128)(2,1)}), bf16[1536,1536]{0,1:T(8,128)(2,1)}) %all-gather.14.cloned.1.call-update) | async-done | bytes 4718608 | tf_op jit(solution)/shard_map/all_gather | solution.py:80
  394.0 5.4 add_convert_fusion.1
  402.7 6.3 fusion.34
  409.1 6.6 bitcast_convert_fusion
  419.3 4.9 reduce-scatter.10.cloned.1.call-done
  427.3 20.8 %reduce-scatter.8.cloned.1.call-done = bf16[2,16,1536]{2,1,0:T(8,128)(2,1)} async-done(((bf16[2,64,1536]{2,1,0:T(8,128)(2,1)}), bf16[2,16,1536]{2,1,0:T(8,128)(2,1)}) %reduce-scatter.8.cloned.1.call-update) | async-done | bytes 98320 | tf_op jit(solution)/shard_map/reduce_scatter | solution.py:125
  451.8 6.6 all_gather.35
  466.9 5.2 convolution_convert_fusion.1
  472.1 9.1 fusion.53
  481.2 10.0 convolution_convert_fusion.2
  497.5 5.4 copy.89
  510.3 13.8 %fusion.26 = f32[1536,768,1]{1,0,2:T(8,128)S(1)} fusion(bf16[2,2048,1536]{2,1,0:T(8,128)(2,1)} %all-gather.6.cloned.1.call-done, bf16[2,2112,384]{2,1,0:T(8,128)(2,1)S(1)} %copy.90, bf16[2,2112,384]{2,1,0:T(8,128)(2,1)} %copy.89), kind=kOutput, calls=%fused_computation.48 | convolution fusion | flops 9676259328 | bytes 23789568 | tf_op jit(solution)/shard_map/icd,ice->de/dot_general | solution.py:168
  528.4 17.2 %convolution_convert_fusion = bf16[2,2048,1536]{2,1,0:T(8,128)(2,1)} fusion(bf16[2,2112,384]{2,1,0:T(8,128)(2,1)S(1)} %copy.90, bf16[2,2112,384]{2,1,0:T(8,128)(2,1)} %copy.89, bf16[1536,384]{1,0:T(8,128)(2,1)} %copy-done.37, bf16[1536,384]{1,0:T(8,128)(2,1)} %copy-done.35), kind=kOutput, calls=%fused_computation.2 | convolution fusion | flops 9687269376 | bytes 21430272 | tf_op jit(solution)/shard_map/ice,de->icd/dot_general | solution.py:175
  559.5 417.6 %all-reduce.8.cloned.1.call-done = (bf16[3,1536,384]{2,1,0:T(8,128)(2,1)}, bf16[384,1536]{1,0:T(8,128)(2,1)}, bf16[1536,1536]{1,0:T(8,128)(2,1)}, bf16[1536,1536]{1,0:T(8,128)(2,1)}) async-done(((bf16[3,1536,384]{2,1,0:T(8,128)(2,1)}, bf16[384,1536]{1,0:T(8,128)(2,1)}, bf16[1536,1536]{1,0:T(8,128)(2,1)}, bf16[1536,1536]{1,0:T(8,128)(2,1)}), (bf16[3,1536,384]{2,1,0:T(8,128)(2,1)}, ...) | async-done | bytes 14155792 | tf_op jit(solution)/shard_map/psum | solution.py:201
  985.4 9.0 multiply_reduce_fusion
  995.7 82.1 %reduce-scatter.14.cloned.1.call-done = bf16[2,512,1536]{2,1,0:T(8,128)(2,1)} async-done(((bf16[2,2048,1536]{2,1,0:T(8,128)(2,1)}), bf16[2,512,1536]{2,1,0:T(8,128)(2,1)}) %reduce-scatter.14.cloned.1.call-update) | async-done | bytes 3145744 | tf_op jit(solution)/shard_map/reduce_scatter | solution.py:177
  1097.5 6.5 psum.53
  1104.0 5.5 convert_element_type.160
  1111.3 5.0 convert_element_type.164
  1121.2 95.5 %all-reduce.6.cloned.1.call-done = (f32[6,1536]{1,0:T(8,128)}, f32[8,1536]{1,0:T(8,128)}) async-done(((f32[6,1536]{1,0:T(8,128)}, f32[8,1536]{1,0:T(8,128)}), (f32[6,1536]{1,0:T(8,128)}, f32[8,1536]{1,0:T(8,128)})) %all-reduce.6.cloned.1.call-update) | async-done | bytes 86032 | tf_op jit(solution)/shard_map/psum | solution.py:206
  (320 shorter events, 172.1 us)
Async XLA Ops:
  7.2 71.5 %all-gather.8.cloned.1.call-start = ((), (), s32[]{:S(2)}) async-start(), calls=%async_computation.6 | async-start | bytes 3981312 | tf_op jit(solution)/shard_map/all_gather | solution.py:77
  9.4 152.1 %all-gather.6.cloned.1.call-start = ((), (), s32[]{:S(2)}) async-start(), calls=%async_computation.5 | async-start | bytes 15728640 | tf_op jit(solution)/shard_map/all_gather | solution.py:93
  17.9 10.4 copy-start.86
  17.9 187.5 %all-gather.10.cloned.1.call-start = ((), (), s32[]{:S(2)}) async-start(), calls=%async_computation.7 | async-start | bytes 1327104 | tf_op jit(solution)/shard_map/all_gather | solution.py:78
  19.6 210.7 %reduce-scatter.6.cloned.1.call-start = ((), (), s32[]{:S(2)}) async-start(), calls=%async_computation.8 | async-start | bytes 983040 | tf_op jit(solution)/shard_map/reduce_scatter | solution.py:119
  19.8 63.2 %copy-start.69 = (f32[2,16]{1,0:T(2,128)}, f32[2,16]{1,0:T(2,128)S(1)}, u32[]{:S(2)}) copy-start(f32[2,16]{1,0:T(2,128)S(1)} %broadcast_multiply_fusion.4) | copy-start | bytes 388
  20.0 63.0 %copy-start.81 = (f32[2,16]{1,0:T(2,128)}, f32[2,16]{1,0:T(2,128)S(1)}, u32[]{:S(2)}) copy-start(f32[2,16]{1,0:T(2,128)S(1)} %multiply_reduce_fusion.9) | copy-start | bytes 388
  20.0 63.0 %copy-start.79 = (f32[2,16]{1,0:T(2,128)}, f32[2,16]{1,0:T(2,128)S(1)}, u32[]{:S(2)}) copy-start(f32[2,16]{1,0:T(2,128)S(1)} %fusion.96) | copy-start | bytes 388
  28.2 55.3 %copy-start.20 = (bf16[2,64,1536]{2,1,0:T(8,128)(2,1)}, bf16[2,64,1536]{2,1,0:T(8,128)(2,1)S(1)}, u32[]{:S(2)}) copy-start(bf16[2,64,1536]{2,1,0:T(8,128)(2,1)S(1)} %all_gather.29) | copy-start | bytes 1179652
  83.1 91.4 %copy-start.35 = (bf16[1536,384]{1,0:T(8,128)(2,1)}, bf16[1536,384]{1,0:T(8,128)(2,1)S(1)}, u32[]{:S(2)}) copy-start(bf16[1536,384]{1,0:T(8,128)(2,1)S(1)} %get-tuple-element.151) | copy-start | bytes 3538948
  83.1 91.4 %copy-start.37 = (bf16[1536,384]{1,0:T(8,128)(2,1)}, bf16[1536,384]{1,0:T(8,128)(2,1)S(1)}, u32[]{:S(2)}) copy-start(bf16[1536,384]{1,0:T(8,128)(2,1)S(1)} %get-tuple-element.152) | copy-start | bytes 3538948
  208.1 105.0 %all-gather.12.cloned.1.call-start = ((), (), s32[]{:S(2)}) async-start(), calls=%async_computation.9 | async-start | bytes 5308416 | tf_op jit(solution)/shard_map/all_gather | solution.py:79
  210.3 183.7 %all-gather.14.cloned.1.call-start = ((), (), s32[]{:S(2)}) async-start(), calls=%async_computation.10 | async-start | bytes 5308416 | tf_op jit(solution)/shard_map/all_gather | solution.py:80
  212.5 211.7 %reduce-scatter.10.cloned.1.call-start = ((), (), s32[]{:S(2)}) async-start(), calls=%async_computation.12 | async-start | bytes 983040 | tf_op jit(solution)/shard_map/reduce_scatter | solution.py:135
  402.7 45.5 %reduce-scatter.8.cloned.1.call-start = ((), (), s32[]{:S(2)}) async-start(), calls=%async_computation.11 | async-start | bytes 491520 | tf_op jit(solution)/shard_map/reduce_scatter | solution.py:125
  409.1 146.4 %reduce-scatter.12.cloned.1.call-start = ((), (), s32[]{:S(2)}) async-start(), calls=%async_computation.13 | async-start | bytes 491520 | tf_op jit(solution)/shard_map/reduce_scatter | solution.py:180
  481.2 11.5 copy-start.59
  510.1 467.1 %all-reduce.8.cloned.1.call-start = ((), (), s32[]{:S(2)}) async-start(), calls=%async_computation.16 | async-start | bytes 28311552 | tf_op jit(solution)/shard_map/psum | solution.py:201
  510.3 13.8 %copy-start.21 = (bf16[2,64,1536]{2,1,0:T(8,128)(2,1)S(1)}, bf16[2,64,1536]{2,1,0:T(8,128)(2,1)}, u32[]{:S(2)}) copy-start(bf16[2,64,1536]{2,1,0:T(8,128)(2,1)} %copy-done.20) | copy-start | bytes 1179652
  510.3 13.8 %copy-start.44 = (bf16[2,64,768]{2,1,0:T(8,128)(2,1)S(1)}, bf16[2,64,768]{2,1,0:T(8,128)(2,1)}, u32[]{:S(2)}) copy-start(bf16[2,64,768]{2,1,0:T(8,128)(2,1)} %copy-done.43) | copy-start | bytes 589828
  528.4 549.5 %reduce-scatter.14.cloned.1.call-start = ((), (), s32[]{:S(2)}) async-start(), calls=%async_computation.14 | async-start | bytes 15728640 | tf_op jit(solution)/shard_map/reduce_scatter | solution.py:177
  545.7 671.1 %all-reduce.6.cloned.1.call-start = ((), (), s32[]{:S(2)}) async-start(), calls=%async_computation.15 | async-start | bytes 196608 | tf_op jit(solution)/shard_map/psum | solution.py:206
  556.6 437.8 %copy-start.84 = (f32[2,16]{1,0:T(2,128)}, f32[2,16]{1,0:T(2,128)S(1)}, u32[]{:S(2)}) copy-start(f32[2,16]{1,0:T(2,128)S(1)} %multiply_multiply_fusion.6) | copy-start | bytes 388
  985.4 92.5 %copy-start.1 = (f32[512,1536]{1,0:T(8,128)S(1)}, f32[512,1536]{1,0:T(8,128)}, u32[]{:S(2)}) copy-start(f32[512,1536]{1,0:T(8,128)} %copy-done) | copy-start | bytes 9437188
  985.4 92.5 %copy-start.49 = (f32[1536]{0:T(1024)S(1)}, f32[1536]{0:T(1024)}, u32[]{:S(2)}) copy-start(f32[1536]{0:T(1024)} %copy-done.48) | copy-start | bytes 18436
  985.4 92.5 %copy-start.57 = (f32[2,512]{1,0:T(2,128)S(1)}, f32[2,512]{1,0:T(2,128)}, u32[]{:S(2)}) copy-start(f32[2,512]{1,0:T(2,128)} %copy-done.56) | copy-start | bytes 12292
  995.7 86.6 %copy-start.68 = (f32[2,512]{1,0:T(2,128)S(1)}, f32[2,512]{1,0:T(2,128)}, u32[]{:S(2)}) copy-start(f32[2,512]{1,0:T(2,128)} %copy-done.67) | copy-start | bytes 12292
  995.7 86.6 %copy-start.61 = (f32[2,512]{1,0:T(2,128)S(1)}, f32[2,512]{1,0:T(2,128)}, u32[]{:S(2)}) copy-start(f32[2,512]{1,0:T(2,128)} %copy-done.60) | copy-start | bytes 12292
  1095.6 15.7 %slice-start.2 = ((s8[4718592]{0:T(1024)(128)(4,1)}), s8[524288]{0:T(1024)(128)(4,1)S(1)}, s32[]{:S(2)}) async-start(s8[4718592]{0:T(1024)(128)(4,1)} %bitcast.104), calls=%async_computation.19 | async-start | bytes 1048576
  1116.3 105.4 %copy-start.19 = (f32[384,192]{1,0:T(8,128)S(1)}, f32[384,192]{1,0:T(8,128)}, u32[]{:S(2)}) copy-start(f32[384,192]{1,0:T(8,128)} %copy.92) | copy-start | bytes 884740
  1116.3 105.4 %copy-start.29 = (f32[384,192]{1,0:T(8,128)S(1)}, f32[384,192]{1,0:T(8,128)}, u32[]{:S(2)}) copy-start(f32[384,192]{1,0:T(8,128)} %copy.93) | copy-start | bytes 884740
  1121.2 104.0 %copy-start.5 = (f32[1536,192]{1,0:T(8,128)S(1)}, f32[1536,192]{1,0:T(8,128)}, u32[]{:S(2)}) copy-start(f32[1536,192]{1,0:T(8,128)} %copy.95) | copy-start | bytes 3538948
  (72 other events, 295.7 us)
Sparse Core Ops, SparseCore 0:
  10.8 67.8 all-gather.7
  80.9 80.5 all-gather.5
  164.3 41.0 all-gather.9
  208.3 22.0 reduce-scatter.5
  233.2 79.8 all-gather.11
  316.0 78.0 all-gather.13
  402.8 21.4 reduce-scatter.9
  427.3 20.7 reduce-scatter.7
  510.2 21.1 reduce-scatter.11
  537.1 440.0 all-reduce.7
  979.7 98.0 reduce-scatter.13
  1095.7 121.0 all-reduce.5
where the time goes:
time: 1280 us; the launch traced here: 1270 us
  waiting for transfers between devices  914 us (71%)
  matrix products  131 us (10%)
  other arithmetic  104 us (8%)
  local copies, waits for them, and re-layouts  64 us (5%)
  blocking collectives  34.9 us (3%)
  between operations  21.2 us (2%)
    psum x1, waiting for transfers between devices, shards(): lax.psum(qkv_part.astype(jnp.bfloat16), 'dp').astype(jnp.float32)  418 us
    psum x1, waiting for transfers between devices, shards(): small_norm, small_time = lax.psum((norm_part, time_part), ('dp', 'mp'))  95.5 us
    reduce_scatter x1, waiting for transfers between devices, shards(): lax.psum_scatter(media_norm_part.astype(jnp.bfloat16), 'mp', scatter_dime...  82.1 us
    all_gather x1, waiting for transfers between devices, shards(): lax.all_gather(media_norm, 'mp', axis=1, tiled=True)  77.9 us
    all_gather x1, waiting for transfers between devices, shards(): lax.all_gather(down_master.astype(half), 'dp', axis=1, tiled=True)  75.8 us
    all_gather x1, waiting for transfers between devices, shards(): lax.all_gather(up_master.astype(half), 'dp', axis=0, tiled=True)  74 us
    all_gather x1, waiting for transfers between devices, shards(): lax.all_gather(qkv_master.astype(half), 'dp', axis=1, tiled=True)  49.8 us
    unnamed x200, local copies, waits for them, and re-layouts  30.2 us
  transfers between devices with their start and end apart: 12, of which 11 were waited for; matrix products, arithmetic and copies ran while one was open for 13% of the time, Pallas kernels for 0%

commit v1 on v0

v1 whole, which is shorter than its diff:
```python
import functools
import math

import jax
import jax.numpy as jnp
from jax import lax
from jax.experimental import pallas as pl
from jax.experimental.pallas import tpu as pltpu
from jax.sharding import PartitionSpec as P

HEAD_DIM = 96
FRAMES = 8
PATCHES = 256


EPS = 1e-05
MOMENT = 0.9
STEP_RATES = (30.0, 1200.0, 120.0, 40.0, 1000.0, 1200.0)
DECAY_AVG = 0.75
HIGH = lax.Precision.HIGHEST
NEGATIVE = -1e30
ROWS_IN_VMEM = 5 * 1024 * 1024


def layer_norm(values, factor, offset):
    centered = values - jnp.mean(values, axis=-1, keepdims=True)
    variance = jnp.mean(centered * centered, axis=-1, keepdims=True)
    return centered * lax.rsqrt(variance + EPS) * factor + offset


def exact_gelu(values):
    return jax.nn.gelu(values, approximate=False)


def square_sum(arrays):
    running = jnp.zeros((), jnp.float32)
    for member in arrays:
        running = running + jnp.sum(member * member)
    return running


def advance(gradient, master, momentum, average, clip_factor, rate):
    clipped = gradient * clip_factor
    moment_new = MOMENT * momentum + clipped
    master_new = master - rate * (clipped + MOMENT * moment_new)
    average_new = DECAY_AVG * average + (1.0 - DECAY_AVG) * master_new
    return (clipped, master_new, moment_new, average_new)


class Place:
    def __init__(self, dp_count, mp_count):
        z_count = 4 if dp_count % 4 == 0 else 1
        c_count = 2 if mp_count % 2 == 0 else 1
        self.size = {
            "z": z_count,
            "x": dp_count // z_count,
            "y": mp_count // c_count,
            "c": c_count,
        }
        self.count = {"dp": dp_count, "mp": mp_count}

    def mine(self):
        dp, mp = lax.axis_index("dp"), lax.axis_index("mp")
        x_count, c_count = self.size["x"], self.size["c"]
        return {
            "z": lax.div(dp, x_count),
            "x": lax.rem(dp, x_count),
            "y": lax.div(mp, c_count),
            "c": lax.rem(mp, c_count),
        }

    def shifted(self, me, axis, step):
        return {**me, axis: lax.rem(me[axis] + step, self.size[axis])}

    def device(self, at):
        return {
            "dp": at["z"] * self.size["x"] + at["x"],
            "mp": at["y"] * self.size["c"] + at["c"],
        }


def region(ref, at, chunk, whole):
    def pick(axis):
        return slice(None) if axis in whole else at[axis]

    return ref.at[pick("y"), pick("c"), chunk[0], pick("z"), pick("x"), chunk[1]]


def remote(src, dst, send, recv, device):
    return pltpu.make_async_remote_copy(
        src_ref=src,
        dst_ref=dst,
        send_sem=send,
        recv_sem=recv,
        device_id=device,
        device_id_type=pl.DeviceIdType.MESH,
    )


def greet(devices):
    barrier = pltpu.get_barrier_semaphore()
    for device in devices:
        pl.semaphore_signal(
            barrier, inc=1, device_id=device, device_id_type=pl.DeviceIdType.MESH
        )
    pl.semaphore_wait(barrier, len(devices))


class Swap:
    def __init__(self, place, axis, spread, value, late=0):
        self.place, self.axis, self.spread, self.value = place, axis, spread, value
        self.late = late
        self.n = place.count[axis]
        shape = value.shape if spread else (self.n,) + value.shape
        self.out = jax.ShapeDtypeStruct(shape, value.dtype)
        self.scratch = [
            pltpu.SemaphoreType.DMA((self.n,)),
            pltpu.SemaphoreType.DMA((self.n,)),
        ]

    def peers(self):
        rank = lax.axis_index(self.axis)
        return [{self.axis: lax.rem(rank + k, self.n)} for k in range(1, self.n)]

    def begin(self, refs):
        self.refs = refs

    def steps(self):
        return self.late + 1

    def own(self):
        src, dst, send, _ = self.refs
        rank = lax.axis_index(self.axis)
        return pltpu.make_async_copy(
            src.at[rank] if self.spread else src, dst.at[rank], send.at[0]
        )

    def copies(self, receive):
        src, dst, send, recv = self.refs
        rank = lax.axis_index(self.axis)
        for k in range(1, self.n):
            there, here = lax.rem(rank + k, self.n), lax.rem(rank + self.n - k, self.n)
            yield remote(
                src.at[there] if self.spread else src,
                dst.at[here if receive else rank],
                send.at[k],
                recv.at[k],
                {self.axis: there},
            )

    def step(self, time):
        if time == self.late:
            self.own().start()
            for copy in self.copies(False):
                copy.start()

    def finish(self):
        self.own().wait()
        for copy in self.copies(False):
            copy.wait_send()
        for copy in self.copies(True):
            copy.wait_recv()


def pair_at(index, chunks):
    return [n for n in (2 * index, 2 * index + 1) if 0 <= n < len(chunks)]


GATHER_STAGES = (0, 2, 1, 3, 4)
REDUCE_STAGES = (4, 3, 2, 1, 0)
ORDERS = (("z", "x", "y", "c"), ("z", "y", "x", "c"))


class Gather:
    def __init__(self, place, value, late=0):
        self.place, self.value, self.late = place, value, late
        s = place.size
        t, h = value.shape[:2]
        self.chunks = [(a, b) for a in range(t) for b in range(h)]
        self.out = jax.ShapeDtypeStruct(
            (s["y"], s["c"], t, s["z"], s["x"], h) + value.shape[2:], value.dtype
        )
        self.most = max(s.values())
        sems = pltpu.SemaphoreType.DMA((len(self.chunks), 5, self.most))
        self.scratch = [sems, sems]

    def peers(self):
        me = self.place.mine()
        return [
            self.place.device(self.place.shifted(me, a, k))
            for a in "zxyc"
            for k in range(1, self.place.size[a])
        ]

    def copies(self, n, stage, receive):
        src, dst, send, recv = self.refs
        order = ORDERS[n % 2]
        axis, whole = order[stage], order[:stage]
        me = self.me
        for k in range(1, self.place.size[axis]):
            there = self.place.shifted(me, axis, k)
            here = self.place.shifted(me, axis, self.place.size[axis] - k)
            at = here if receive else me
            block = (
                src.at[self.chunks[n][0], self.chunks[n][1]]
                if stage == 0
                else region(dst, me, self.chunks[n], whole)
            )
            yield remote(
                block,
                region(dst, at, self.chunks[n], whole),
                send.at[n, stage, k],
                recv.at[n, stage, k],
                self.place.device(there),
            )

    def begin(self, refs):
        self.refs, self.me = refs, self.place.mine()

    def own(self, n):
        src, dst, send, _ = self.refs
        chunk = self.chunks[n]
        return pltpu.make_async_copy(
            src.at[chunk[0], chunk[1]], region(dst, self.me, chunk, ()), send.at[n, 4, 0]
        )

    def steps(self):
        return self.late + pl.cdiv(len(self.chunks), 2) + 4

    def step(self, time):
        for stage in GATHER_STAGES:
            for n in pair_at(time - self.late - stage, self.chunks):
                if stage == 0:
                    self.own(n).start()
                if stage == 1:
                    self.own(n).wait()
                if stage > 0:
                    for copy in self.copies(n, stage - 1, True):
                        copy.wait_recv()
                if stage < 4:
                    for copy in self.copies(n, stage, False):
                        copy.start()

    def finish(self):
        for n in range(len(self.chunks)):
            for stage in range(4):
                for copy in self.copies(n, stage, False):
                    copy.wait_send()


BACK_ORDERS = (("c", "y", "x", "z"), ("c", "x", "y", "z"))
LAYOUT = ("y", "z", "x")


class Reduce:
    def __init__(self, place, value, late=0, starts=None, kept=None):
        self.place, self.value = place, value
        s = place.size
        t, h = value.shape[2], value.shape[5]
        tail = value.shape[6:]
        self.chunks = [(a, b) for a in range(t) for b in range(h)]
        self.out = jax.ShapeDtypeStruct((t, h) + tail, jnp.float32)
        count = len(self.chunks)
        pairs = pl.cdiv(count, 2)
        self.starts = [late + k for k in range(pairs)] if starts is None else starts
        self.kept = count if kept is None else min(kept, count)
        sems = pltpu.SemaphoreType.DMA((count, 5, max(s.values())))
        full = tuple(s[a] for a in LAYOUT)
        held = pltpu.VMEM((self.kept,) + full + tail, value.dtype)
        self.scratch = [sems, sems, held, held]
        self.spots = {}
        for parity in range(min(2, count)):
            mine = (count + 1 - parity) // 2
            left = list(LAYOUT)
            for stage, axis in list(enumerate(BACK_ORDERS[parity]))[1:]:
                left.remove(axis)
                shape = (mine, max(s[axis] - 1, 1)) + tuple(s[a] for a in left) + tail
                self.spots[parity, stage] = len(self.scratch)
                self.scratch.append(pltpu.VMEM(shape, value.dtype))
        self.out_spot = len(self.scratch)
        self.scratch.append(pltpu.VMEM((t, h) + tail, jnp.float32))
        self.scratch.append(pltpu.SemaphoreType.DMA((1,)))
        self.scratch.append(pltpu.SemaphoreType.REGULAR)

    peers = Gather.peers

    def part(self, n, stage, at):
        order = BACK_ORDERS[n % 2]
        if stage == 0:
            t, h = self.chunks[n]
            return self.src.at[:, at, t, :, :, h]
        index = tuple(
            at if a == order[stage] else self.me[a] if a in order[:stage] else slice(None)
            for a in LAYOUT
        )
        return self.scr[2].at[(n % self.kept,) + index]

    def into(self, n, stage):
        if stage == 0:
            return self.scr[3].at[pl.ds(n % self.kept, 1)]
        return self.scr[self.spots[n % 2, stage]].at[n // 2]

    def copies(self, n, stage):
        axis = BACK_ORDERS[n % 2][stage]
        for k in range(1, self.place.size[axis]):
            there = self.place.shifted(self.me, axis, k)
            yield remote(
                self.part(n, stage, there[axis]),
                self.into(n, stage).at[k - 1],
                self.scr[0].at[n, stage, k],
                self.scr[1].at[n, stage, k],
                self.place.device(there),
            )

    def own(self, n):
        t, h = self.chunks[n]
        return pltpu.make_async_copy(
            self.src.at[:, self.me["c"], t, :, :, h],
            self.scr[2].at[n % self.kept],
            self.scr[0].at[n, 4, 0],
        )

    def begin(self, refs):
        self.src, self.dst, self.scr = refs[0], refs[1], refs[2:]
        self.me = self.place.mine()

    def steps(self):
        return self.starts[-1] + 5

    def add(self, n, stage):
        order = BACK_ORDERS[n % 2]
        axis = order[stage]
        count = self.place.size[axis] - 1
        into = self.into(n, stage)
        sizes = [self.place.size[a] for a in LAYOUT if a not in order[: stage + 1]]
        if stage == 0:
            base = target = self.scr[2].at[n % self.kept]
        else:
            base = target = self.part(n, stage, self.me[axis])
        if stage == 3:
            target = self.scr[self.out_spot].at[self.chunks[n][0], self.chunks[n][1]]

        def one(flat, carry):
            index = []
            rest = flat
            for size in reversed(sizes):
                index.insert(0, lax.rem(rest, size))
                rest = lax.div(rest, size)
            index = tuple(index) + (Ellipsis,)
            if count == 1 and target.dtype == base.dtype:
                target[index] = base[index] + into[(0,) + index]
                return carry
            value = base[index].astype(jnp.float32)
            for k in range(count):
                value = value + into[(k,) + index].astype(jnp.float32)
            target[index] = value.astype(target.dtype)
            return carry

        total = math.prod(sizes)
        if total == 1:
            one(jnp.int32(0), 0)
        else:
            lax.fori_loop(0, total, one, 0)

    def step(self, time):
        for stage in REDUCE_STAGES:
            for pair, start in enumerate(self.starts):
                if start + stage == time:
                    self.advance(pair, stage)

    def advance(self, pair, stage):
        sibling = self.place.device(self.place.shifted(self.me, "c", 1))
        reused = len(self.chunks) > self.kept and self.place.size["c"] > 1
        for n in pair_at(pair, self.chunks):
            if stage == 0:
                if n >= self.kept:
                    for old in range(4):
                        for copy in self.copies(n - self.kept, old):
                            copy.wait_send()
                    if reused:
                        pl.semaphore_wait(self.scr[-1], 1)
                self.own(n).start()
            if stage == 1:
                self.own(n).wait()
            if stage > 0:
                for copy in self.copies(n, stage - 1):
                    copy.wait_recv()
                self.add(n, stage - 1)
            if stage == 1 and reused and n + self.kept < len(self.chunks):
                pl.semaphore_signal(
                    self.scr[-1],
                    inc=1,
                    device_id=sibling,
                    device_id_type=pl.DeviceIdType.MESH,
                )
            if stage < 4:
                for copy in self.copies(n, stage):
                    copy.start()

    def finish(self):
        out = pltpu.make_async_copy(self.scr[self.out_spot], self.dst, self.scr[-2].at[0])
        out.start()
        for n in range(max(0, len(self.chunks) - self.kept), len(self.chunks)):
            for stage in range(4):
                for copy in self.copies(n, stage):
                    copy.wait_send()
        out.wait()


class Total:
    AXES = ("c", "y", "x", "z")

    def __init__(self, place, value):
        self.place, self.value = place, value
        self.out = jax.ShapeDtypeStruct(value.shape, value.dtype)
        sems = pltpu.SemaphoreType.DMA((4, max(place.size.values())))
        self.scratch = [sems, sems] + [
            pltpu.VMEM((place.size[a],) + value.shape, value.dtype) for a in self.AXES
        ]

    peers = Gather.peers

    def begin(self, refs):
        self.src, self.dst, self.send, self.recv = refs[:4]
        self.bufs = refs[4:]
        self.me = self.place.mine()

    def copies(self, stage, receive):
        axis = self.AXES[stage]
        size = self.place.size[axis]
        buf, me = self.bufs[stage], self.me
        for k in range(1, size):
            there = self.place.shifted(me, axis, k)
            here = self.place.shifted(me, axis, size - k)
            yield remote(
                buf.at[me[axis]],
                buf.at[here[axis] if receive else me[axis]],
                self.send.at[stage, k],
                self.recv.at[stage, k],
                self.place.device(there),
            )

    def advance(self, stage):
        if stage == 0:
            value = self.src[...]
        else:
            for copy in self.copies(stage - 1, True):
                copy.wait_recv()
            for copy in self.copies(stage - 1, False):
                copy.wait_send()
            value = self.bufs[stage - 1][0]
            for k in range(1, self.place.size[self.AXES[stage - 1]]):
                value = value + self.bufs[stage - 1][k]
        if stage == 4:
            self.dst[...] = value
            return
        self.bufs[stage][self.me[self.AXES[stage]]] = value
        for copy in self.copies(stage, False):
            copy.start()


def norm_back(value, factor, pulled):
    centered = value - jnp.mean(value, axis=-1, keepdims=True)
    variance = jnp.mean(centered * centered, axis=-1, keepdims=True)
    scale = lax.rsqrt(variance + EPS)
    unit = centered * scale
    inner = pulled * factor
    back = scale * (
        inner
        - jnp.mean(inner, axis=-1, keepdims=True)
        - unit * jnp.mean(inner * unit, axis=-1, keepdims=True)
    )
    return (
        back,
        jnp.sum(pulled * unit, axis=0, keepdims=True),
        jnp.sum(pulled, axis=0, keepdims=True),
    )


def communicate(label, number, parts):
    count = len(parts)

    def kernel(*refs):
        ins, outs, rest = refs[:count], refs[count : 2 * count], refs[2 * count :]
        devices, seen = [], set()
        for part in parts:
            kind = part.axis if isinstance(part, Swap) else "grid"
            if kind not in seen:
                seen.add(kind)
                devices += part.peers()
        greet(devices)
        spot = 0
        for part, src, dst in zip(parts, ins, outs):
            size = len(part.scratch)
            part.begin((src, dst) + tuple(rest[spot : spot + size]))
            spot += size
        staged = parts
        for time in range(max([part.steps() for part in staged], default=0)):
            for part in staged:
                part.step(time)
        for part in parts:
            part.finish()

    return pl.pallas_call(
        kernel,
        out_shape=[part.out for part in parts],
        in_specs=[pl.BlockSpec(memory_space=pl.ANY)] * count,
        out_specs=[pl.BlockSpec(memory_space=pl.ANY)] * count,
        scratch_shapes=[s for part in parts for s in part.scratch],
        compiler_params=pltpu.CompilerParams(
            collective_id=number, has_side_effects=True, vmem_limit_bytes=58 * 1024 * 1024
        ),
        name=label,
    )(*[part.value for part in parts])


def product(left, right, dims):
    return lax.dot_general(left, right, (dims, ((), ())), preferred_element_type=jnp.float32)


NN, NT, TN = ((1,), (0,)), ((1,), (1,)), ((0,), (0,))


def spread_heads(rows, heads):
    owner = lax.broadcasted_iota(jnp.int32, rows.shape, 1)
    kept = [
        jnp.where((owner >= h * HEAD_DIM) & (owner < (h + 1) * HEAD_DIM), rows, 0)
        for h in range(heads)
    ]
    return jnp.concatenate(kept, axis=0)


def fold_heads(wide, heads):
    rows = wide.shape[0] // heads
    owner = lax.broadcasted_iota(jnp.int32, (rows, wide.shape[1]), 1)
    out = wide[:rows]
    for h in range(1, heads):
        out = jnp.where(owner >= h * HEAD_DIM, wide[h * rows : (h + 1) * rows], out)
    return out


def as_row(column):
    wide = jnp.broadcast_to(column, (column.shape[0], 128))
    return jnp.transpose(wide)[:1]


def as_column(row):
    return jnp.transpose(jnp.broadcast_to(row, (128, row.shape[1])))[:, :1]


def front_kernel(place, heads, scale, halves_w, parts, *refs):
    half, f32 = jnp.bfloat16, jnp.float32
    own_w, cot, lat_in, media, keep, time_rows, norms = refs[:7]
    w_o, back_o, src_o, lat_o, q_o, p_o, blend_o, mixed_o, stat_o = refs[7:16]
    w_vm, lat_vm, src_vm, q_vm, p_vm, blend_vm, mixed_vm, stat_vm, sems = refs[16:25]
    rest = list(refs[25:])
    gather_w, gather_c, lat_swap, mixed_swap, stat_swap = parts
    ends = (
        (own_w, w_vm),
        (cot, back_o),
        (lat_in, lat_vm),
        (mixed_vm, mixed_o),
        (stat_vm, stat_o),
    )
    for part, end in zip(parts, ends):
        size = len(part.scratch)
        part.begin(end + tuple(rest[:size]))
        rest = rest[size:]
    items, slots, width = media.shape
    lat_own = lat_in.shape[1]
    blocks, block = q_vm.shape[0], q_vm.shape[3]
    lat_total = blocks * lat_own
    c_count = place.size["c"]
    mp_rank = lax.axis_index("mp")
    greet(gather_w.peers() + lat_swap.peers())
    clock = [0]

    def run_to(time):
        while clock[0] <= time:
            for part in (lat_swap, gather_w, gather_c):
                part.step(clock[0])
            clock[0] += 1

    def arrived(t):
        return 4 + ((t + 1) * halves_w - 1) // 2

    def weight(j, t):
        return w_vm[lax.div(j, c_count), lax.rem(j, c_count), t].reshape(width, block)

    kept = []

    def keep_copy(src, dst):
        copy = pltpu.make_async_copy(src, dst, sems.at[len(kept)])
        copy.start()
        kept.append(copy)

    run_to(0)
    step_rows = math.gcd(64, slots)
    per_item = slots // step_rows

    def norm_media(k, carry):
        item, first = lax.div(k, per_item), lax.rem(k, per_item) * step_rows
        first = pl.multiple_of(first, step_rows)
        frame = lax.div(mp_rank * slots + first, PATCHES)
        value = media[item, pl.ds(first, step_rows)].astype(f32) + time_rows[pl.ds(frame, 1)]
        value = layer_norm(value, norms[0:1], norms[1:2])
        src_vm[item, pl.ds(first, step_rows)] = value.astype(half)
        return carry

    lax.fori_loop(0, items * per_item, norm_media, 0)
    src_vm[:, slots:] = lat_in[...]
    keep_copy(src_vm, src_o)
    run_to(3)
    lat_swap.finish()
    keep_copy(lat_vm, lat_o)
    run_to(arrived(0))

    def ask(j, carry):
        rows = jnp.concatenate(
            [lat_vm[:, n].reshape(lat_total, width) for n in range(items)], axis=0
        )
        query = product(rows, weight(j, 0), NN).astype(half)
        q_vm[j] = query.reshape(items, lat_total, block)
        return carry

    lax.fori_loop(0, blocks, ask, 0)
    keep_copy(q_vm, q_o)
    run_to(arrived(1))

    def score(k, carry):
        j, n = lax.div(k, items), lax.rem(k, items)
        source = src_vm[n]
        reach = product(spread_heads(q_vm[j, n], heads), weight(j, 1), NT).astype(half)
        value = product(reach, source, NT) * scale
        value = jnp.where(keep[n] > 0, value, NEGATIVE)
        peak = jnp.max(value, axis=1, keepdims=True)
        raised = jnp.exp(value - peak)
        total = jnp.sum(raised, axis=1, keepdims=True)
        low = raised.astype(half)
        p_vm[j, n] = low
        blend_vm[j, n] = product(low, source, NN).astype(half)
        stat_vm[j, n, 0:1] = as_row(peak)
        stat_vm[j, n, 1:2] = as_row(total)
        return carry

    lax.fori_loop(0, blocks * items // 2, score, 0)
    run_to(max(arrived(1) + 1, arrived(2)))
    lax.fori_loop(blocks * items // 2, blocks * items, score, 0)
    keep_copy(p_vm, p_o)
    keep_copy(blend_vm, blend_o)

    def mix(k, carry):
        j, n = lax.div(k, items), lax.rem(k, items)
        value = fold_heads(product(blend_vm[j, n], weight(j, 2), NN), heads)
        mixed_vm[:, j, n] = value.reshape(blocks, lat_own, block)
        return carry

    lax.fori_loop(0, blocks * items, mix, 0)
    mixed_swap.step(0)
    stat_swap.step(0)
    run_to(arrived(3))
    keep_copy(w_vm, w_o)
    run_to(gather_c.steps())
    for part in parts:
        if part is not lat_swap:
            part.finish()
    for copy in kept:
        copy.wait()


def front(
    place, own_weights, cot, latent_norm, media, keep, time_rows, norms, heads, scale
):
    half, f32 = jnp.bfloat16, jnp.float32
    items, slots, width = media.shape
    lat_own = latent_norm.shape[1]
    blocks, block = place.count["mp"], own_weights.shape[3]
    lat, keys = blocks * lat_own, slots + lat_own
    rows = heads * lat
    halves_w = own_weights.shape[1]
    late = 2 * halves_w
    mixed = jax.ShapeDtypeStruct((blocks, blocks, items, lat_own, block), f32)
    stats = jax.ShapeDtypeStruct((blocks, items, 2, rows), f32)
    parts = [
        Gather(place, own_weights),
        Gather(place, cot, late),
        Swap(place, "mp", False, latent_norm),
        Swap(place, "mp", True, mixed),
        Swap(place, "mp", False, stats),
    ]
    shapes = [
        parts[0].out,
        parts[2].out,
        jax.ShapeDtypeStruct((items, keys, width), half),
        jax.ShapeDtypeStruct((blocks, items, lat, block), half),
        jax.ShapeDtypeStruct((blocks, items, rows, keys), half),
        jax.ShapeDtypeStruct((blocks, items, rows, width), half),
        mixed,
        stats,
    ]
    scratch = [pltpu.VMEM(shape.shape, shape.dtype) for shape in shapes]
    scratch.append(pltpu.SemaphoreType.DMA((8,)))
    for part in parts:
        scratch += part.scratch
    whole = pl.BlockSpec(memory_space=pltpu.VMEM)
    hbm = pl.BlockSpec(memory_space=pl.ANY)
    return pl.pallas_call(
        functools.partial(front_kernel, place, heads, scale, halves_w, parts),
        in_specs=[hbm, hbm, whole, whole, whole, whole, whole],
        out_specs=[hbm] * 9,
        out_shape=[
            parts[0].out,
            parts[1].out,
            shapes[2],
            parts[2].out,
            shapes[3],
            shapes[4],
            shapes[5],
            parts[3].out,
            parts[4].out,
        ],
        scratch_shapes=scratch,
        compiler_params=pltpu.CompilerParams(
            collective_id=1, has_side_effects=True, vmem_limit_bytes=64 * 1024 * 1024 - 65536
        ),
        name="front",
    )(own_weights, cot, latent_norm, media, keep, time_rows, norms)


def feed_kernel(place, parts, *refs):
    half, f32 = jnp.bfloat16, jnp.float32
    own_rows, up_in, down_in, back_rows, after_attn, cot, mixed, norms, weights = refs[:9]
    (norm_o, ffn_o, up_o, down_o, back_o, term_o, after_o, low_o, sums_o) = refs[9:18]
    (rows_vm, up_vm, down_vm, share_a, share_b, up_give, down_give, w_out) = refs[18:26]
    (hid_vm, pre_vm, mixed_vm, term_vm, sem) = refs[26:31]
    rest = list(refs[31:])
    gather, up_swap, down_swap, first, second, up_back, down_back, back_swap, term_swap = parts
    ends = (
        (own_rows, rows_vm),
        (up_in, up_vm),
        (down_in, down_vm),
        (share_a, norm_o),
        (share_b, ffn_o),
        (up_give, up_o),
        (down_give, down_o),
        (mixed_vm, back_o),
        (term_vm, term_o),
    )
    for part, end in zip(parts, ends):
        size = len(part.scratch)
        part.begin(end + tuple(rest[:size]))
        rest = rest[size:]
    c_count, blocks = place.size["c"], place.count["mp"]
    width, units = norms.shape[1], hid_vm.shape[2]
    greet(gather.peers() + up_swap.peers() + back_swap.peers())
    out_weight = pltpu.make_async_copy(weights.at[:, 3], w_out, sem.at[0])
    gather.step(0)
    up_swap.step(0)
    down_swap.step(0)
    out_weight.start()
    for time in range(1, gather.steps()):
        gather.step(time)
    up_swap.finish()
    down_swap.finish()

    def inner(m, carry):
        y, c = lax.div(m, c_count), lax.rem(m, c_count)
        w_up, w_down = up_vm[...].reshape(width, units), down_vm[...].reshape(width, units)
        rows = rows_vm[y, c].reshape(-1, width)
        pre = product(rows, w_up, NN)
        pulled = product(back_rows[y, c].reshape(-1, width), w_down, NN)
        chance = 0.5 * (1.0 + lax.erf(pre * math.sqrt(0.5)))
        slope = chance + pre * jnp.exp(-0.5 * pre * pre) * math.sqrt(0.5 / math.pi)
        hid_vm[m] = (pre * chance).astype(half)
        pre_back = (pulled * slope).astype(half)
        pre_vm[m] = pre_back
        share = product(pre_back, w_up, NT).astype(half)
        share_a[y, c] = share.reshape(share_a.shape[2:])
        return carry

    lax.fori_loop(0, blocks, inner, 0)
    first.step(0)

    def outer(m, carry):
        y, c = lax.div(m, c_count), lax.rem(m, c_count)
        share = product(hid_vm[m], down_vm[...].reshape(width, units), NT).astype(half)
        share_b[y, c] = share.reshape(share_b.shape[2:])
        return carry

    lax.fori_loop(0, blocks, outer, 0)
    first.step(1)
    second.step(0)
    give = product(rows_vm[...].reshape(-1, width), pre_vm[...].reshape(-1, units), TN)
    up_give[...] = give.astype(half).reshape(up_give.shape)
    give = product(back_rows[...].reshape(-1, width), hid_vm[...].reshape(-1, units), TN)
    down_give[...] = give.astype(half).reshape(down_give.shape)
    first.step(2)
    second.step(1)
    up_back.step(0)
    down_back.step(0)
    first.step(3)
    second.step(2)
    first.step(4)
    pulled = first.scr[first.out_spot]
    factors = jnp.zeros((1, width), f32)
    offsets = jnp.zeros((1, width), f32)
    for t in range(after_attn.shape[0]):
        value, factor, offset = norm_back(after_attn[t], norms[4:5], pulled[t, 0])
        value = cot[t] + value
        after_o[t] = value
        low_o[t] = value.astype(half)
        factors += factor
        offsets += offset
    sums_o[0:1] = factors
    sums_o[1:2] = offsets
    out_weight.wait()
    low = low_o[...].reshape(-1, width)
    heads = term_vm.shape[2]
    for j in range(blocks):
        back = product(low, w_out[j].reshape(width, -1), NN).astype(half)
        mixed_vm[j] = back
        both = mixed[j] * back.astype(f32)
        owner = lax.broadcasted_iota(jnp.int32, both.shape, 1)
        place_of = lax.broadcasted_iota(jnp.int32, (both.shape[0], heads), 1)
        terms = jnp.zeros((both.shape[0], heads), f32)
        for h in range(heads):
            mine = (owner >= h * HEAD_DIM) & (owner < (h + 1) * HEAD_DIM)
            term = jnp.sum(jnp.where(mine, both, 0.0), axis=1, keepdims=True)
            terms = jnp.where(place_of == h, term, terms)
        term_vm[j] = terms
    back_swap.step(0)
    term_swap.step(0)
    second.step(3)
    second.step(4)
    for part in (gather, first, second, up_back, down_back, back_swap, term_swap):
        part.finish()


def feed(place, own_rows, up_pieces, down_pieces, back_rows, after_attn, cot, mixed, norms, weights):
    half, f32 = jnp.bfloat16, jnp.float32
    gather = Gather(place, own_rows)
    rows = gather.out
    width = norms.shape[1]
    blocks, flat, block = mixed.shape
    heads = block // HEAD_DIM
    units = up_pieces.shape[2]
    per = math.prod(rows.shape[2:7])
    mixed_back = jax.ShapeDtypeStruct(mixed.shape, half)
    terms = jax.ShapeDtypeStruct((blocks, flat, heads), f32)
    parts = [
        gather,
        Swap(place, "dp", True, up_pieces),
        Swap(place, "dp", True, down_pieces),
        Reduce(place, rows),
        Reduce(place, rows),
        Swap(place, "dp", True, up_pieces),
        Swap(place, "dp", True, down_pieces),
        Swap(place, "mp", False, mixed_back),
        Swap(place, "mp", False, terms),
    ]
    scratch = [
        pltpu.VMEM(rows.shape, half),
        pltpu.VMEM(up_pieces.shape, half),
        pltpu.VMEM(down_pieces.shape, half),
        pltpu.VMEM(rows.shape, half),
        pltpu.VMEM(rows.shape, half),
        pltpu.VMEM(up_pieces.shape, half),
        pltpu.VMEM(down_pieces.shape, half),
        pltpu.VMEM(weights.shape[:1] + weights.shape[2:], half),
        pltpu.VMEM((blocks, per, units), half),
        pltpu.VMEM((blocks, per, units), half),
        pltpu.VMEM(mixed.shape, half),
        pltpu.VMEM(terms.shape, f32),
        pltpu.SemaphoreType.DMA((1,)),
    ]
    for part in parts:
        scratch += part.scratch
    whole = pl.BlockSpec(memory_space=pltpu.VMEM)
    hbm = pl.BlockSpec(memory_space=pl.ANY)
    return pl.pallas_call(
        functools.partial(feed_kernel, place, parts),
        in_specs=[hbm, hbm, hbm] + [whole] * 5 + [hbm],
        out_specs=[hbm] * 6 + [whole] * 3,
        out_shape=[part.out for part in parts[3:]]
        + [
            jax.ShapeDtypeStruct(after_attn.shape, f32),
            jax.ShapeDtypeStruct(after_attn.shape, half),
            jax.ShapeDtypeStruct((2, width), f32),
        ],
        scratch_shapes=scratch,
        compiler_params=pltpu.CompilerParams(
            collective_id=3, has_side_effects=True, vmem_limit_bytes=60 * 1024 * 1024
        ),
        name="feed",
    )(own_rows, up_pieces, down_pieces, back_rows, after_attn, cot, mixed, norms, weights)


def feed_apart(place, own_rows, up_pieces, down_pieces, back_rows, after_attn, cot, mixed, norms, weights):
    half, f32 = jnp.bfloat16, jnp.float32
    width, units = norms.shape[1], up_pieces.shape[2]
    dot = functools.partial(jnp.einsum, preferred_element_type=f32)
    ffn_rows, up_pieces, down_pieces = communicate(
        "rows",
        3,
        [
            Gather(place, own_rows),
            Swap(place, "dp", True, up_pieces, 1),
            Swap(place, "dp", True, down_pieces, 1),
        ],
    )
    shape, pieces_shape = ffn_rows.shape, up_pieces.shape
    w_up, w_down = up_pieces.reshape(width, units), down_pieces.reshape(width, units)
    ffn_rows, back_rows = ffn_rows.reshape(-1, width), back_rows.reshape(-1, width)
    pre_act = dot("rd,df->rf", ffn_rows, w_up)
    hidden = exact_gelu(pre_act).astype(half)
    hidden_back = dot("rd,df->rf", back_rows, w_down)
    pre_back = jax.vjp(exact_gelu, pre_act)[1](hidden_back)[0].astype(half)
    norm_part = dot("rf,df->rd", pre_back, w_up).astype(half)
    ffn_part = dot("rf,df->rd", hidden, w_down).astype(half)
    down_part = dot("rd,rf->df", back_rows, hidden).astype(half)
    up_part = dot("rd,rf->df", ffn_rows, pre_back).astype(half)
    norm_pulled, ffn_out, up_owned, down_owned = communicate(
        "ffn",
        4,
        [
            Reduce(place, norm_part.reshape(shape)),
            Reduce(place, ffn_part.reshape(shape)),
            Swap(place, "dp", True, up_part.reshape(pieces_shape), 1),
            Swap(place, "dp", True, down_part.reshape(pieces_shape), 1),
        ],
    )
    pull = jax.vjp(layer_norm, after_attn, norms[4], norms[5])[1]
    through, factor, offset = pull(norm_pulled.reshape(after_attn.shape))
    after_back = cot + through
    low = after_back.astype(half)
    mixed_back = dot("ld,jde->jle", low.reshape(-1, width), weights[:, 3]).astype(half)
    terms = jnp.sum(
        (mixed * mixed_back.astype(f32)).reshape(*mixed.shape[:2], -1, HEAD_DIM), axis=-1
    )
    mixed_rows, terms = communicate(
        "back", 5, [Swap(place, "mp", False, mixed_back), Swap(place, "mp", False, terms)]
    )
    sums = jnp.stack([factor, offset])
    return (
        norm_pulled,
        ffn_out,
        up_owned,
        down_owned,
        mixed_rows,
        terms,
        after_back,
        low,
        sums,
    )


def attend_back_kernel(place, heads, scale, reduce, latent_swap, totals, *refs):
    half, f32 = jnp.bfloat16, jnp.float32
    (src, lat, q, p, blend, back, mix, low, row, wq, wk, wv, up_vm, down_vm) = refs[:14]
    (media, time_rows, norms, latents, after_back, ffn_sums) = refs[14:20]
    (grad_o, media_o, owned_o, latents_o, small_o, square_o) = refs[20:26]
    (acc, lat_acc, lat_vm, kept, stage_a, stage_b, small, square, stage_sem) = refs[26:35]
    rest = list(refs[35:])
    phase, block = pl.program_id(0), pl.program_id(1)
    blocks = pl.num_programs(1)
    items = src.shape[0]
    lat_total = lat.shape[1]
    width = src.shape[2]
    for part, give, out in (
        (reduce, grad_o, owned_o),
        (latent_swap, lat_acc, lat_vm),
        (totals[0], small, small_o),
        (totals[1], square, square_o),
    ):
        size = len(part.scratch)
        part.begin((give, out) + tuple(rest[:size]))
        rest = rest[size:]

    def at(number, index, action):
        pl.when((phase == number) & (block == index))(action)

    last = place.count["mp"] - 1
    plan, moves_1, moves_2 = reduce_plan(len(reduce.chunks), place.count["mp"], items)
    c_count = place.size["c"]
    y_of, c_of = lax.div(block, c_count), lax.rem(block, c_count)

    def staged(t, buffer, number):
        return pltpu.make_async_copy(buffer, grad_o.at[y_of, c_of, t], stage_sem.at[number])

    def hand_over(first, first_value, second, second_value):
        @pl.when(block > 0)
        def _():
            staged(first, stage_a, 0).wait()
            staged(second, stage_b, 1).wait()

        stage_a[...] = first_value.astype(half).reshape(stage_a.shape)
        stage_b[...] = second_value.astype(half).reshape(stage_b.shape)
        staged(first, stage_a, 0).start()
        staged(second, stage_b, 1).start()

        @pl.when(block == last)
        def _():
            staged(first, stage_a, 0).wait()
            staged(second, stage_b, 1).wait()

    def column(item, which):
        return as_column(row[0, item, which : which + 1])

    at(0, 0, lambda: greet(latent_swap.peers() + reduce.peers()))

    @pl.when(phase == 0)
    def _():
        back_s = jnp.concatenate(
            [
                (spread_heads(back[0, n], heads) * column(n, 0)).astype(half)
                for n in range(items)
            ],
            axis=0,
        )
        value_grad = product(blend[0].reshape(back_s.shape[0], width), back_s, TN)
        out_grad = product(
            low[...].reshape(-1, width), mix[0].reshape(-1, mix.shape[3]), TN
        )
        hand_over(3, out_grad, 2, value_grad)

    def events(number, half_step):
        for (where, point), moves in plan.items():
            if where == number and point % items == half_step:

                def carry_out(moves=moves):
                    for move in moves:
                        reduce.advance(*move)

                at(where, point // items, carry_out)

    at(1, 0, lambda: reduce.advance(0, 0))

    @pl.when(phase == 1)
    def _():
        turns, queries, query_backs = [], [], []
        for n in range(items):
            back_s = spread_heads(back[0, n], heads)
            pull = product(back_s, wv[0, 0], NT).astype(half)
            prob_back = product(pull, src[n], NT)
            score_back = (
                p[0, n].astype(jnp.float32) * (column(n, 0) * scale) * (prob_back - column(n, 1))
            ).astype(half)
            kept[block, n] = score_back
            turn = product(score_back, src[n], NN).astype(half)
            query_back = fold_heads(product(turn, wk[0, 0], NN), heads).astype(half)
            latent_back = product(query_back, wq[0, 0], NT)
            latent_back = latent_back.reshape(lat_acc.shape[0], -1, width)

            @pl.when(block == 0)
            def _():
                lat_acc[:, n] = latent_back

            @pl.when(block > 0)
            def _():
                lat_acc[:, n] += latent_back

            turns.append(turn)
            queries.append(spread_heads(q[0, n], heads))
            query_backs.append(query_back)
            if n + 1 < items:
                events(1, n)
        key_grad = product(
            jnp.concatenate(turns, axis=0), jnp.concatenate(queries, axis=0), TN
        )
        query_grad = product(
            lat[...].reshape(items * lat_total, width), jnp.concatenate(query_backs, axis=0), TN
        )
        hand_over(1, key_grad, 0, query_grad)

    events(1, items - 1)
    at(1, last, lambda: latent_swap.step(0))

    @pl.when(phase == 2)
    def _():
        for n in range(items):
            pull = product(spread_heads(back[0, n], heads), wv[0, 0], NT)
            reach = product(spread_heads(q[0, n], heads), wk[0, 0], NT)
            value = product(
                jnp.concatenate([kept[block, n], p[0, n]], axis=0),
                jnp.concatenate([reach.astype(half), (pull * column(n, 0)).astype(half)], axis=0),
                TN,
            )

            @pl.when(block == 0)
            def _():
                acc[n] = value

            @pl.when(block > 0)
            def _():
                acc[n] += value

            if n + 1 < items:
                events(2, n)

    events(2, items - 1)

    slots = media.shape[1]
    step_rows = math.gcd(64, slots)
    per_item = slots // step_rows
    mp_rank = lax.axis_index("mp")

    def media_back(k, carry):
        item, first = lax.div(k, per_item), lax.rem(k, per_item) * step_rows
        first = pl.multiple_of(first, step_rows)
        frame = lax.div(mp_rank * slots + first, PATCHES)
        value = media[item, pl.ds(first, step_rows)].astype(f32) + time_rows[pl.ds(frame, 1)]
        back, factor, offset = norm_back(
            value, norms[0:1], acc[item, pl.ds(first, step_rows)]
        )
        acc[item, pl.ds(first, step_rows)] = back
        small[0:1] += factor
        small[1:2] += offset
        small[pl.ds(6 + frame, 1)] += jnp.sum(back, axis=0, keepdims=True)
        return carry

    def end():
        small[...] = jnp.zeros_like(small)
        half_way = items * per_item // 2
        lax.fori_loop(0, half_way, media_back, 0)
        for move in moves_1:
            reduce.advance(*move)
        lax.fori_loop(half_way, items * per_item, media_back, 0)
        out = pltpu.make_async_copy(acc.at[:, pl.ds(0, slots)], media_o, stage_sem.at[0])
        out.start()
        latent_swap.finish()
        for n in range(items):
            pulled = acc[n, slots:]
            for k in range(lat_vm.shape[0]):
                pulled = pulled + lat_vm[k, n]
            value, factor, offset = norm_back(latents[n], norms[2:3], pulled)
            latents_o[n] = after_back[n] + value
            small[2:3] += factor
            small[3:4] += offset
        small[4:6] = ffn_sums[...]
        totals[0].advance(0)
        totals[0].advance(1)
        reduce.advance(*moves_2[0])
        totals[0].advance(2)
        for move in moves_2[1:-1]:
            reduce.advance(*move)
        totals[0].advance(3)
        sums = jnp.zeros((1, 1), f32)
        for buffer in (up_vm, down_vm):
            for k in range(buffer.shape[0]):
                value = buffer[k].astype(f32)
                sums = sums + jnp.sum(value * value, keepdims=True)
        reduce.advance(*moves_2[-1])
        totals[0].advance(4)
        owned = reduce.scr[reduce.out_spot]
        for t in range(owned.shape[0]):
            for h in range(owned.shape[1]):
                value = owned[t, h]
                sums = sums + jnp.sum(value * value, keepdims=True)
        square[...] = jnp.broadcast_to(sums, square.shape)
        totals[1].advance(0)
        reduce.finish()
        for stage in range(1, 5):
            totals[1].advance(stage)
        out.wait()

    at(2, last, end)


def attend_back(
    place,
    source,
    latent_rows,
    query,
    chance,
    blend,
    back,
    mixed,
    low,
    rows_in,
    weights,
    owned_ffn,
    rows_end,
    weight_halves,
    heads,
    scale,
):
    items, keys, width = source.shape
    lat = latent_rows.shape[1]
    own = low.shape[1]
    blocks, block = weights.shape[0], weights.shape[3]
    rows = heads * lat
    half, f32 = jnp.bfloat16, jnp.float32
    s = place.size
    part = width // (s["z"] * s["x"] * weight_halves)
    inner = (s["z"], s["x"], weight_halves, part, block)
    grad = jax.ShapeDtypeStruct((s["y"], s["c"], 4) + inner, half)
    lat_shares = jax.ShapeDtypeStruct((blocks, items, own, width), f32)
    order = [3, 2, 1, 0]
    reduce = Reduce(place, grad, kept=6 if weight_halves == 2 else 2)
    reduce.chunks = [(t, h) for t in order for h in range(weight_halves)]
    latent_swap = Swap(place, "mp", True, lat_shares)
    small = jax.ShapeDtypeStruct((16, width), f32)
    square = jax.ShapeDtypeStruct((8, 128), f32)
    totals = [Total(place, small), Total(place, square)]
    slots = keys - own

    def weight(t, first):
        return pl.BlockSpec(
            (1, 1, width, block), lambda ph, j: (j * jnp.minimum(ph // first, 1), t, 0, 0)
        )

    def per(*shape):
        return pl.BlockSpec((1, items) + shape, lambda ph, j: (j,) + (0,) * (1 + len(shape)))

    def early(*shape):
        return pl.BlockSpec(
            (1, items) + shape,
            lambda ph, j: (j + (blocks - 1 - j) * jnp.minimum(ph, 1),) + (0,) * (1 + len(shape)),
        )

    def late(*shape):
        return pl.BlockSpec(
            (1, items) + shape,
            lambda ph, j: (j * jnp.minimum(ph, 1),) + (0,) * (1 + len(shape)),
        )

    whole = pl.BlockSpec(memory_space=pltpu.VMEM)
    hbm = pl.BlockSpec(memory_space=pl.ANY)
    scratch = [
        pltpu.VMEM((items, keys, width), f32),
        pltpu.VMEM(lat_shares.shape, f32),
        pltpu.VMEM(lat_shares.shape, f32),
        pltpu.VMEM((blocks, items, rows, keys), half),
        pltpu.VMEM(inner, half),
        pltpu.VMEM(inner, half),
        pltpu.VMEM(small.shape, f32),
        pltpu.VMEM(square.shape, f32),
        pltpu.SemaphoreType.DMA((2,)),
    ]
    for member in [reduce, latent_swap] + totals:
        scratch += member.scratch
    return pl.pallas_call(
        functools.partial(
            attend_back_kernel, place, heads, scale, reduce, latent_swap, totals
        ),
        grid=(3, blocks),
        in_specs=[
            whole,
            whole,
            late(lat, block),
            late(rows, keys),
            early(rows, width),
            per(lat, block),
            early(own, block),
            whole,
            per(2, rows),
            weight(0, 1),
            weight(1, 1),
            weight(2, 1),
        ]
        + [whole] * 8,
        out_specs=[hbm] * 3 + [whole] * 3,
        out_shape=[
            grad,
            jax.ShapeDtypeStruct((items, slots, width), f32),
            reduce.out,
            jax.ShapeDtypeStruct((items, own, width), f32),
            small,
            square,
        ],
        scratch_shapes=scratch,
        compiler_params=pltpu.CompilerParams(
            collective_id=6, has_side_effects=True, vmem_limit_bytes=64 * 1024 * 1024 - 65536
        ),
        name="attend_back",
    )(
        source,
        latent_rows,
        query,
        chance,
        blend,
        back,
        mixed,
        low,
        rows_in,
        weights,
        weights,
        weights,
        *owned_ffn,
        *rows_end,
    )


def reduce_plan(chunks, blocks, items):
    points = blocks * items
    if chunks == 8:
        eighths = {
            (1, 0): [(0, 1), (1, 0)],
            (1, 3): [(0, 2), (1, 1)],
            (1, 6): [(0, 3), (1, 2)],
            (1, 7): [(2, 0)],
            (2, 0): [(2, 1), (1, 3)],
            (2, 2): [(0, 4), (3, 0)],
            (2, 4): [(3, 1)],
            (2, 6): [(2, 2)],
        }
    else:
        eighths = {
            (1, 0): [(0, 1)],
            (1, 3): [(0, 2)],
            (1, 6): [(0, 3)],
            (1, 7): [(0, 4), (1, 0)],
            (2, 0): [(1, 1)],
        }
    plan = {
        (phase, (eighth + 1) * points // 8 - 1): moves for (phase, eighth), moves in eighths.items()
    }
    if chunks == 8:
        return plan, ((1, 4), (3, 2), (2, 3)), ((3, 3), (2, 4), (3, 4))
    return plan, ((1, 2),), ((1, 3), (1, 4))


def refresh_kernel(rates, *refs):
    f32 = jnp.float32
    count = len(rates)
    square, small = refs[:2]
    ins, outs = refs[2 : 2 + 4 * count], refs[2 + 4 * count :]
    total = square[0:1, 0:1] + jnp.sum(small[...] * small[...], keepdims=True)
    norm = jnp.sqrt(total)
    outs[0][...] = norm
    clip = 1.0 / jnp.maximum(norm, 1.0)
    spot = 1
    for n, rate in enumerate(rates):
        grad, master, momentum, average = ins[4 * n : 4 * n + 4]
        with_copy = n < 4
        into = outs[spot : spot + (5 if with_copy else 4)]
        spot += len(into)
        rows = grad.shape[0]
        step = math.gcd(rows, 32)

        def update(at):
            done = advance(
                grad[at].astype(f32), master[at], momentum[at], average[at], clip, rate
            )
            for ref, value in zip(into, done):
                ref[at] = value
            if with_copy:
                into[4][at] = done[1].astype(jnp.bfloat16)

        if step < 16:
            update(Ellipsis)
        else:

            def one(k, carry):
                update(pl.ds(pl.multiple_of(k * step, step), step))
                return carry

            lax.fori_loop(0, rows // step, one, 0)


def refresh(square, small, groups):
    f32 = jnp.float32
    whole = pl.BlockSpec(memory_space=pltpu.VMEM)
    shapes = [jax.ShapeDtypeStruct((1, 1), f32)]
    for n, (rate, grad, *_) in enumerate(groups):
        shapes += [jax.ShapeDtypeStruct(grad.shape, f32)] * 4
        if n < 4:
            shapes.append(jax.ShapeDtypeStruct(grad.shape, jnp.bfloat16))
    arrays = [array for _, *four in groups for array in four]
    return pl.pallas_call(
        functools.partial(refresh_kernel, [rate for rate, *_ in groups]),
        in_specs=[whole] * (2 + len(arrays)),
        out_specs=[whole] * len(shapes),
        out_shape=shapes,
        compiler_params=pltpu.CompilerParams(vmem_limit_bytes=60 * 1024 * 1024),
        name="refresh",
    )(square, small, *arrays)


def halves(rows):
    return 2 if rows % 32 == 0 else 1


def shards(
    latents,
    media,
    frames,
    cotangent,
    qkv_master,
    qkv_momentum,
    qkv_average,
    out_master,
    out_momentum,
    out_average,
    up_master,
    up_momentum,
    up_average,
    down_master,
    down_momentum,
    down_average,
    norm_params,
    norm_momentum,
    norm_average,
    time_table,
    time_momentum,
    time_average,
):
    f32 = jnp.float32
    half = jnp.bfloat16
    mp_rank = lax.axis_index("mp")
    mp_count = lax.axis_size("mp")
    dp_count = lax.axis_size("dp")
    place = Place(dp_count, mp_count)
    items, lat_own, width = latents.shape
    lat_total = lat_own * mp_count
    slots = media.shape[1]
    block = qkv_master.shape[2]
    rows_d = qkv_master.shape[1]
    heads = block // HEAD_DIM
    hidden_block = up_master.shape[1]
    units = hidden_block // dp_count
    own_rows = items * lat_own
    all_rows = dp_count * mp_count * own_rows
    scale_factor = HEAD_DIM ** (-0.5)
    dot = functools.partial(jnp.einsum, preferred_element_type=f32)

    def as_chunks(rows):
        t = halves(own_rows)
        return rows.reshape(t, 1, own_rows // t, width)

    weight_halves = halves(rows_d)
    own_weights = jnp.concatenate(
        [qkv_master.astype(half), out_master.astype(half).T[None]], axis=0
    ).reshape(4, weight_halves, rows_d // weight_halves, block)
    latent_norm = layer_norm(latents, norm_params[2], norm_params[3]).astype(half)

    def as_pieces(wide):
        return wide.reshape(rows_d, dp_count, units).transpose(1, 0, 2)

    def from_pieces(pieces):
        return pieces.transpose(1, 0, 2).reshape(rows_d, hidden_block)

    up_pieces = as_pieces(up_master.astype(half))
    down_pieces = as_pieces(down_master.T.astype(half))
    slot_ids = mp_rank * slots + jnp.arange(slots)
    frame_ids = slot_ids // PATCHES
    keep = jnp.concatenate(
        [frame_ids[None, :] < frames[:, None], jnp.ones((items, lat_own), jnp.bool_)], axis=1
    )
    (
        weights,
        back_rows,
        source,
        latent_rows,
        queries,
        chances,
        blends,
        mixed_blocks,
        stats,
    ) = front(
        place,
        own_weights,
        as_chunks(cotangent.astype(half)),
        latent_norm,
        media,
        keep.astype(f32)[:, None],
        time_table,
        norm_params,
        heads,
        scale_factor,
    )
    weights = weights.reshape(mp_count, 4, width, block)
    w_out = weights[:, 3]
    latent_rows = latent_rows.transpose(1, 0, 2, 3).reshape(items, lat_total, width)
    part_peaks, part_sums = stats[:, :, :, 0], stats[:, :, :, 1]
    grow = jnp.exp(part_peaks - jnp.max(part_peaks, axis=0))
    shares = grow / jnp.sum(part_sums * grow, axis=0)
    share = lax.dynamic_index_in_dim(shares, mp_rank, 0, keepdims=False)
    own_shares = lax.dynamic_slice_in_dim(
        shares.reshape(mp_count, mp_count, items, heads, lat_total), mp_rank * lat_own, lat_own, 4
    )
    own_shares = jnp.repeat(own_shares.transpose(0, 1, 2, 4, 3), HEAD_DIM, axis=-1)
    mixed_full = jnp.sum(mixed_blocks * own_shares, axis=0)
    mixed_j = mixed_full.astype(half)
    after_attn = latents + dot("jile,jde->ild", mixed_j, w_out)
    ffn_norm = layer_norm(after_attn, norm_params[4], norm_params[5]).astype(half)
    t = halves(own_rows)
    by_chunk = (t, own_rows // t, width)
    (
        _,
        ffn_out,
        up_owned,
        down_owned,
        mixed_back_rows,
        row_terms,
        after_back,
        attn_low,
        ffn_sums,
    ) = (feed if 2 * all_rows * width <= ROWS_IN_VMEM else feed_apart)(
        place,
        as_chunks(ffn_norm),
        up_pieces,
        down_pieces,
        back_rows,
        after_attn.reshape(by_chunk),
        cotangent.reshape(by_chunk),
        mixed_full.reshape(mp_count, own_rows, block),
        norm_params,
        weights,
    )
    latents_out = after_attn + ffn_out.reshape(latents.shape)
    after_back, attn_low = after_back.reshape(latents.shape), attn_low.reshape(latents.shape)
    row_terms = row_terms.reshape(mp_count, mp_count, items, lat_own, heads)
    row_terms = row_terms.transpose(1, 2, 4, 0, 3).reshape(mp_count, items, heads * lat_total)
    back_j = (
        mixed_back_rows.reshape(mp_count, mp_count, items, lat_own, block)
        .transpose(1, 2, 0, 3, 4)
        .reshape(mp_count, items, lat_total, block)
    )
    _, media_grad, owned, latents_grad, small, square = attend_back(
        place,
        source,
        latent_rows,
        queries,
        chances,
        blends,
        back_j,
        mixed_j,
        attn_low,
        jnp.stack([share, row_terms], axis=2),
        weights,
        [up_owned, down_owned],
        [media, time_table, norm_params, latents, after_back, ffn_sums],
        weight_halves,
        heads,
        scale_factor,
    )
    owned = owned.reshape(4, rows_d, block)
    qkv_shape = (3 * rows_d, block)
    groups = [
        (
            STEP_RATES[0],
            owned[:3].reshape(qkv_shape),
            qkv_master.reshape(qkv_shape),
            qkv_momentum.reshape(qkv_shape),
            qkv_average.reshape(qkv_shape),
        ),
        (STEP_RATES[1], owned[3], out_master.T, out_momentum.T, out_average.T),
        (STEP_RATES[2], from_pieces(up_owned), up_master, up_momentum, up_average),
        (
            STEP_RATES[3],
            from_pieces(down_owned),
            down_master.T,
            down_momentum.T,
            down_average.T,
        ),
        (STEP_RATES[4], small[:6], norm_params, norm_momentum, norm_average),
        (STEP_RATES[5], small[6:14], time_table, time_momentum, time_average),
    ]
    (
        grad_norm,
        qkv_grad,
        qkv_new,
        qkv_momentum_new,
        qkv_average_new,
        qkv_copy,
        out_grad,
        out_new,
        out_momentum_new,
        out_average_new,
        out_copy,
        up_grad,
        up_new,
        up_momentum_new,
        up_average_new,
        up_copy,
        down_grad,
        down_new,
        down_momentum_new,
        down_average_new,
        down_copy,
        norm_grad,
        norm_new,
        norm_momentum_new,
        norm_average_new,
        time_grad,
        time_new,
        time_momentum_new,
        time_average_new,
    ) = refresh(square, small, groups)
    grad_norm = grad_norm.reshape(())
    out_grad, out_new, out_momentum_new, out_average_new, out_copy = (
        value.T for value in (out_grad, out_new, out_momentum_new, out_average_new, out_copy)
    )
    down_grad, down_new, down_momentum_new, down_average_new, down_copy = (
        value.T for value in (down_grad, down_new, down_momentum_new, down_average_new, down_copy)
    )
    qkv_grad, qkv_new, qkv_momentum_new, qkv_average_new, qkv_copy = (
        value.reshape(qkv_master.shape)
        for value in (qkv_grad, qkv_new, qkv_momentum_new, qkv_average_new, qkv_copy)
    )
    return (
        latents_out,
        latents_grad,
        media_grad,
        grad_norm,
        qkv_grad,
        qkv_new,
        qkv_momentum_new,
        qkv_average_new,
        out_grad,
        out_new,
        out_momentum_new,
        out_average_new,
        up_grad,
        up_new,
        up_momentum_new,
        up_average_new,
        down_grad,
        down_new,
        down_momentum_new,
        down_average_new,
        norm_grad,
        norm_new,
        norm_momentum_new,
        norm_average_new,
        time_grad,
        time_new,
        time_momentum_new,
        time_average_new,
        qkv_copy,
        out_copy,
        up_copy,
        down_copy,
    )


def solution(mesh):
    placed = (
        P("dp", "mp", None),
        P("dp", "mp", None),
        P("dp"),
        P("dp", "mp", None),
        P(None, "dp", "mp"),
        P(None, "dp", "mp"),
        P(None, "dp", "mp"),
        P("mp", "dp"),
        P("mp", "dp"),
        P("mp", "dp"),
        P("dp", "mp"),
        P("dp", "mp"),
        P("dp", "mp"),
        P("mp", "dp"),
        P("mp", "dp"),
        P("mp", "dp"),
        P(),
        P(),
        P(),
        P(),
        P(),
        P(),
    )
    return jax.shard_map(
        shards,
        mesh=mesh,
        in_specs=placed,
        out_specs=(
            P("dp", "mp", None),
            P("dp", "mp", None),
            P("dp", "mp", None),
            P(),
            P(None, "dp", "mp"),
            P(None, "dp", "mp"),
            P(None, "dp", "mp"),
            P(None, "dp", "mp"),
            P("mp", "dp"),
            P("mp", "dp"),
            P("mp", "dp"),
            P("mp", "dp"),
            P("dp", "mp"),
            P("dp", "mp"),
            P("dp", "mp"),
            P("dp", "mp"),
            P("mp", "dp"),
            P("mp", "dp"),
            P("mp", "dp"),
            P("mp", "dp"),
            P(),
            P(),
            P(),
            P(),
            P(),
            P(),
            P(),
            P(),
            P(None, "dp", "mp"),
            P("mp", "dp"),
            P("dp", "mp"),
            P("mp", "dp"),
        ),
        check_vma=False,
    )
```

time: 1280 us -> 475 us (0.37)
  waiting for transfers between devices: 914 us -> 0 us
  Pallas kernels: 0 us -> 427 us
  matrix products: 131 us -> 3.95 us
  other arithmetic: 104 us -> 10.9 us
  blocking collectives: 34.9 us -> 0 us
  local copies, waits for them, and re-layouts: 64 us -> 31.3 us
  between operations: 21.2 us -> 0.94 us
    psum x2 -> x0, waiting for transfers between devices: 513 us -> none  [the longest x1 418 us: shards(): lax.psum(qkv_part.astype(jnp.bfloat16), 'dp').astype(jnp.float32)]
    pallas_call x0 -> x4, Pallas kernels: none -> 427 us  [the longest x1 155 us: attend_back(): pl.pallas_call(functools.partial(attend_back_kernel, place, heads, scale,...]
    all_gather x5 -> x0, waiting for transfers between devices: 283 us -> none  [the longest x1 77.9 us: shards(): lax.all_gather(media_norm, 'mp', axis=1, tiled=True)]
    dot_general x25 -> x1, matrix products: 125 us -> 3.95 us  [shards(): after_attn = latents + dot('jile,jde->ild', mixed_j, w_out)]
    reduce_scatter x5 -> x0, waiting for transfers between devices: 118 us -> none  [the longest x1 82.1 us: shards(): lax.psum_scatter(media_norm_part.astype(jnp.bfloat16), 'mp', scatter_dime...]
    convert_element_type x15 -> x4, other arithmetic: 40.2 us -> 0.15 us  [the longest x1 0.06 us: shards(): up_pieces = as_pieces(up_master.astype(half))]
    reduce_sum x11 -> x2, other arithmetic: 35.5 us -> 0.15 us  [the longest x1 0.1 us: shards(): mixed_full = jnp.sum(mixed_blocks * own_shares, axis=0)]
    all_gather x4 -> x0, blocking collectives: 28.4 us -> none  [the longest x1 8.11 us: shards(): lax.all_gather(latent_norm, 'mp', axis=1, tiled=True)]
  transfers between devices with their start and end apart: 12 -> 0, of which waited for: 11 -> 0; matrix products, arithmetic and copies ran while one was open for 13% -> 0% of each run, Pallas kernels for 0% -> 0%
where the time goes in v1:
time: 475 us; the launch traced here: 474 us
  Pallas kernels  427 us (90%)
  local copies, waits for them, and re-layouts  31.3 us (7%)
  other arithmetic  10.9 us (2%)
    pallas_call x1, Pallas kernels, attend_back(): pl.pallas_call(functools.partial(attend_back_kernel, place, heads, scale,...  155 us
    pallas_call x1, Pallas kernels, feed(): pl.pallas_call(functools.partial(feed_kernel, place, parts), in_specs=[hb...  131 us
    pallas_call x1, Pallas kernels, front(): pl.pallas_call(functools.partial(front_kernel, place, heads, scale, halve...  129 us
    pallas_call x1, Pallas kernels, refresh(): pl.pallas_call(functools.partial(refresh_kernel, [rate for rate, *_ in gr...  12.9 us

profile of v1, /device:TPU:0, one launch (start us, length us, event | category | flops | bytes accessed | tf_op | source)
XLA Modules:
  0.0 474.3 jit_solution(16616604690091626506)
XLA Ops:
  0.7 1.1 reduce_sum.54
  1.8 1.1 multiply_reduce_fusion.2
  2.9 0.7 broadcast_compare_fusion
  4.3 1.6 slice_reduce_fusion.1
  5.9 1.7 add_convert_fusion.1.refs_2_
  7.6 1.6 convert_bitcast_fusion.refs_1_
  9.3 0.9 pad_maximum_fusion.refs_0_
  10.7 0.6 reshape.206
  12.0 0.6 reshape.207
  12.6 1.5 copy_bitcast_fusion
  14.1 128.9 %front.1 = (bf16[2,2,4,4,2,2,96,384]{7,6,5,4,3,2,1,0:T(8,128)(2,1)}, bf16[2,2,2,4,2,1,16,1536]{7,6,5,4,3,2,1,0:T(8,128)(2,1)}, bf16[2,528,1536]{2,1,0:T(8,128)(2...) custom-call(bf16[4,2,96,384]{3,2,1,0:T(8,128)(2,1)} %pad_maximum_fus, ...), custom_call_target="tpu_custom_call" | custom-call | tf_op jit(solution)/shard_map/front/pallas_call | solution.py:707
  143.0 0.9 slice.38
  144.0 0.9 copy.64
  145.7 0.8 copy.70
  147.6 0.6 copy-done.10
  148.4 0.8 copy-done.1
  149.2 4.0 fusion.13
  153.4 0.7 fusion.3.refs_0_
  154.1 130.6 %feed.1 = (f32[2,1,16,1536]{3,2,1,0:T(8,128)}, f32[2,1,16,1536]{3,2,1,0:T(8,128)}, bf16[8,192,192]{2,1,0:T(8,128)(2,1)}, bf16[8,192,192]{2,1,0:T(8,128)(2,1)}, b...) custom-call(bf16[2,1,16,1536]{3,2,1,0:T(8,128)(2,1)} %fusion.3.refs_, ...), custom_call_target="tpu_custom_call" | custom-call | tf_op jit(solution)/shard_map/feed/pallas_call | solution.py:880
  284.7 1.8 bitcast_add_fusion
  286.5 1.8 copy.71
  288.7 0.6 pad_maximum_fusion.1.refs_8_
  289.3 154.8 %attend_back.1 = (bf16[2,2,4,4,2,2,96,384]{7,6,5,4,3,2,1,0:T(8,128)(2,1)}, f32[2,512,1536]{2,1,0:T(8,128)}, f32[4,2,96,384]{3,2,1,0:T(8,128)}, f32[2,16,1536]{2,...) custom-call(bf16[2,528,1536]{2,1,0:T(8,128)(2,1)} %get-tuple-element.88.refs_0_, bf16[2,64,1536]{2,1,0:T(8,128)(2,1)} %bitcast.98, ...), custom_call_target="tpu_custom_call" | custom-call | tf_op jit(solution)/shard_map/attend_back/pallas_call | solution.py:1242
  444.1 1.5 slice.45.refs_22_
  445.6 1.4 slice.44.refs_18_
  447.0 1.8 slice.43
  448.8 2.1 slice.42
  451.4 1.5 reshape.219.refs_14_
  453.3 1.5 reshape.218.refs_10_
  454.8 12.9 %refresh.1 = (f32[1,1]{1,0:T(1,128)}, f32[576,384]{1,0:T(8,128)}, f32[576,384]{1,0:T(8,128)}, f32[576,384]{1,0:T(8,128)}, f32[576,384]{1,0:T(8,128)}, /*index=5*...) custom-call(f32[8,128]{1,0:T(8,128)} %get-tuple-element.102.refs_0_,, ...), custom_call_target="tpu_custom_call" | custom-call | tf_op jit(solution)/shard_map/refresh/pallas_call | solution.py:1370
  467.7 0.7 copy.83
  468.4 5.9 %copy.84 = f32[2,512,1536]{2,1,0:T(8,128)} copy(f32[2,512,1536]{2,1,0:T(8,128)} %get-tuple-element.182) | data formatting | bytes 12582912
  (60 shorter events, 5.5 us)
Async XLA Ops:
  0.7 8.5 %copy-start.8 = (f32[384,192]{0,1:T(8,128)S(1)}, f32[384,192]{0,1:T(8,128)}, u32[]{:S(2)}) copy-start(f32[384,192]{0,1:T(8,128)} %param.29) | copy-start | bytes 884740
  0.7 8.5 %copy-start.4 = (f32[3,192,384]{2,1,0:T(8,128)S(1)}, f32[3,192,384]{2,1,0:T(8,128)}, u32[]{:S(2)}) copy-start(f32[3,192,384]{2,1,0:T(8,128)} %param.26) | copy-start | bytes 2654212
  9.2 1.5 copy-start.3
  10.7 1.3 copy-start.2
  143.0 2.7 copy-start.11
  147.1 1.1 copy-start.10
  148.3 0.9 copy-start.1
  148.4 4.8 %copy-start.7 = (f32[4,2,16,384]{3,2,1,0:T(8,128)}, f32[4,2,16,384]{3,2,1,0:T(8,128)S(1)}, u32[]{:S(2)}) copy-start(f32[4,2,16,384]{3,2,1,0:T(8,128)S(1)} %multiply_reduce_fusion) | copy-start | bytes 589828
  149.2 4.0 copy-start.9
  149.2 4.2 copy-start.14
  149.2 4.2 copy-start.15
  153.2 1.0 copy-start
  284.7 3.6 copy-start.12
  447.0 3.9 copy-start.6
  450.9 2.0 copy-start.5
  454.8 12.9 %copy-start.13 = (f32[2,16,1536]{2,1,0:T(8,128)S(1)}, f32[2,16,1536]{2,1,0:T(8,128)}, u32[]{:S(2)}) copy-start(f32[2,16,1536]{2,1,0:T(8,128)} %get-tuple-element.181) | copy-start | bytes 589828

commit v2 on v1

--- a/solution.py
+++ b/solution.py
@@ -19,6 +19,7 @@
 DECAY_AVG = 0.75
 HIGH = lax.Precision.HIGHEST
 NEGATIVE = -1e30
+SWAP_AT = 5
 ROWS_IN_VMEM = 5 * 1024 * 1024
 
 
@@ -550,34 +551,36 @@
 
 def front_kernel(place, heads, scale, halves_w, parts, *refs):
     half, f32 = jnp.bfloat16, jnp.float32
-    own_w, cot, lat_in, media, keep, time_rows, norms = refs[:7]
-    w_o, back_o, src_o, lat_o, q_o, p_o, blend_o, mixed_o, stat_o = refs[7:16]
-    w_vm, lat_vm, src_vm, q_vm, p_vm, blend_vm, mixed_vm, stat_vm, sems = refs[16:25]
-    rest = list(refs[25:])
-    gather_w, gather_c, lat_swap, mixed_swap, stat_swap = parts
+    qkv, out_t, cot_in, latents, ffn_in, media, keep, time_rows, norms = refs[:9]
+    w_o, back_o, src_o, lat_o, q_o, p_o, blend_o, mixed_o, stat_o, ffn_o = refs[9:19]
+    w_vm, lat_vm, src_vm, q_vm, p_vm, blend_vm, mixed_vm, stat_vm, sems = refs[19:28]
+    own_w, cot, lat_in = refs[28:31]
+    rest = list(refs[31:])
+    gather_w, gather_c, lat_swap, mixed_swap, stat_swap, ffn_swap = parts
     ends = (
         (own_w, w_vm),
         (cot, back_o),
         (lat_in, lat_vm),
         (mixed_vm, mixed_o),
         (stat_vm, stat_o),
+        (ffn_in, ffn_o),
     )
     for part, end in zip(parts, ends):
         size = len(part.scratch)
         part.begin(end + tuple(rest[:size]))
         rest = rest[size:]
     items, slots, width = media.shape
-    lat_own = lat_in.shape[1]
+    lat_own = latents.shape[1]
     blocks, block = q_vm.shape[0], q_vm.shape[3]
     lat_total = blocks * lat_own
     c_count = place.size["c"]
     mp_rank = lax.axis_index("mp")
-    greet(gather_w.peers() + lat_swap.peers())
+    greet(gather_w.peers() + lat_swap.peers() + ffn_swap.peers())
     clock = [0]
 
     def run_to(time):
         while clock[0] <= time:
-            for part in (lat_swap, gather_w, gather_c):
+            for part in (lat_swap, gather_w, gather_c, ffn_swap):
                 part.step(clock[0])
             clock[0] += 1
 
@@ -594,7 +597,13 @@
         copy.start()
         kept.append(copy)
 
+    for n in range(items):
+        lat_in[n] = layer_norm(latents[n], norms[2:3], norms[3:4]).astype(half)
+    for t in range(4):
+        value = qkv[t] if t < 3 else out_t[...]
+        own_w[t] = value.astype(half).reshape(own_w.shape[1:])
     run_to(0)
+    cot[...] = cot_in[...].astype(half)
     step_rows = math.gcd(64, slots)
     per_item = slots // step_rows
 
@@ -669,24 +678,28 @@
 
 
 def front(
-    place, own_weights, cot, latent_norm, media, keep, time_rows, norms, heads, scale
+    place, qkv, out_t, cot, latents, ffn_pieces, media, keep, time_rows, norms, halves_w, heads, scale
 ):
     half, f32 = jnp.bfloat16, jnp.float32
     items, slots, width = media.shape
-    lat_own = latent_norm.shape[1]
-    blocks, block = place.count["mp"], own_weights.shape[3]
+    lat_own = latents.shape[1]
+    rows_d, block = out_t.shape
+    blocks = place.count["mp"]
+    own_weights = jax.ShapeDtypeStruct((4, halves_w, rows_d // halves_w, block), half)
+    low_cot = jax.ShapeDtypeStruct(cot.shape, half)
+    latent_norm = jax.ShapeDtypeStruct(latents.shape, half)
     lat, keys = blocks * lat_own, slots + lat_own
     rows = heads * lat
-    halves_w = own_weights.shape[1]
     late = 2 * halves_w
     mixed = jax.ShapeDtypeStruct((blocks, blocks, items, lat_own, block), f32)
     stats = jax.ShapeDtypeStruct((blocks, items, 2, rows), f32)
     parts = [
         Gather(place, own_weights),
-        Gather(place, cot, late),
+        Gather(place, low_cot, late),
         Swap(place, "mp", False, latent_norm),
         Swap(place, "mp", True, mixed),
         Swap(place, "mp", False, stats),
+        Swap(place, "dp", True, ffn_pieces, SWAP_AT),
     ]
     shapes = [
         parts[0].out,
@@ -700,14 +713,15 @@
     ]
     scratch = [pltpu.VMEM(shape.shape, shape.dtype) for shape in shapes]
     scratch.append(pltpu.SemaphoreType.DMA((8,)))
+    scratch += [pltpu.VMEM(v.shape, half) for v in (own_weights, low_cot, latent_norm)]
     for part in parts:
         scratch += part.scratch
     whole = pl.BlockSpec(memory_space=pltpu.VMEM)
     hbm = pl.BlockSpec(memory_space=pl.ANY)
     return pl.pallas_call(
         functools.partial(front_kernel, place, heads, scale, halves_w, parts),
-        in_specs=[hbm, hbm, whole, whole, whole, whole, whole],
-        out_specs=[hbm] * 9,
+        in_specs=[whole] * 4 + [hbm] + [whole] * 4,
+        out_specs=[hbm] * 10,
         out_shape=[
             parts[0].out,
             parts[1].out,
@@ -718,31 +732,28 @@
             shapes[5],
             parts[3].out,
             parts[4].out,
+            parts[5].out,
         ],
         scratch_shapes=scratch,
         compiler_params=pltpu.CompilerParams(
             collective_id=1, has_side_effects=True, vmem_limit_bytes=64 * 1024 * 1024 - 65536
         ),
         name="front",
-    )(own_weights, cot, latent_norm, media, keep, time_rows, norms)
+    )(qkv, out_t, cot, latents, ffn_pieces, media, keep, time_rows, norms)
 
 
 def feed_kernel(place, parts, *refs):
     half, f32 = jnp.bfloat16, jnp.float32
-    own_rows, up_in, down_in, back_rows, after_attn, cot, mixed, norms, weights = refs[:9]
-    (norm_o, ffn_o, up_o, down_o, back_o, term_o, after_o, low_o, sums_o) = refs[9:18]
-    (rows_vm, up_vm, down_vm, share_a, share_b, up_give, down_give, w_out) = refs[18:26]
-    (hid_vm, pre_vm, mixed_vm, term_vm, sem) = refs[26:31]
-    rest = list(refs[31:])
-    gather, up_swap, down_swap, first, second, up_back, down_back, back_swap, term_swap = parts
+    own_rows, pieces, back_rows, after_attn, cot, mixed, norms, weights = refs[:8]
+    (norm_o, ffn_o, back_o, term_o, give_o, after_o, low_o, sums_o) = refs[8:16]
+    (rows_vm, up_vm, down_vm, share_a, share_b, w_out) = refs[16:22]
+    (hid_vm, pre_vm, mixed_vm, term_vm, sem) = refs[22:27]
+    rest = list(refs[27:])
+    gather, first, second, back_swap, term_swap = parts
     ends = (
         (own_rows, rows_vm),
-        (up_in, up_vm),
-        (down_in, down_vm),
         (share_a, norm_o),
         (share_b, ffn_o),
-        (up_give, up_o),
-        (down_give, down_o),
         (mixed_vm, back_o),
         (term_vm, term_o),
     )
@@ -752,20 +763,18 @@
         rest = rest[size:]
     c_count, blocks = place.size["c"], place.count["mp"]
     width, units = norms.shape[1], hid_vm.shape[2]
-    greet(gather.peers() + up_swap.peers() + back_swap.peers())
+    greet(gather.peers() + back_swap.peers())
     out_weight = pltpu.make_async_copy(weights.at[:, 3], w_out, sem.at[0])
     gather.step(0)
-    up_swap.step(0)
-    down_swap.step(0)
     out_weight.start()
+    up_vm[...] = pieces[:, :, :units].reshape(width, units)
+    down_vm[...] = pieces[:, :, units:].reshape(width, units)
     for time in range(1, gather.steps()):
         gather.step(time)
-    up_swap.finish()
-    down_swap.finish()
 
     def inner(m, carry):
         y, c = lax.div(m, c_count), lax.rem(m, c_count)
-        w_up, w_down = up_vm[...].reshape(width, units), down_vm[...].reshape(width, units)
+        w_up, w_down = up_vm[...], down_vm[...]
         rows = rows_vm[y, c].reshape(-1, width)
         pre = product(rows, w_up, NN)
         pulled = product(back_rows[y, c].reshape(-1, width), w_down, NN)
@@ -783,7 +792,7 @@
 
     def outer(m, carry):
         y, c = lax.div(m, c_count), lax.rem(m, c_count)
-        share = product(hid_vm[m], down_vm[...].reshape(width, units), NT).astype(half)
+        share = product(hid_vm[m], down_vm[...], NT).astype(half)
         share_b[y, c] = share.reshape(share_b.shape[2:])
         return carry
 
@@ -791,13 +800,12 @@
     first.step(1)
     second.step(0)
     give = product(rows_vm[...].reshape(-1, width), pre_vm[...].reshape(-1, units), TN)
-    up_give[...] = give.astype(half).reshape(up_give.shape)
+    half_shape = give_o.shape[:2] + (units,)
+    give_o[:, :, :units] = give.astype(half).reshape(half_shape)
     give = product(back_rows[...].reshape(-1, width), hid_vm[...].reshape(-1, units), TN)
-    down_give[...] = give.astype(half).reshape(down_give.shape)
+    give_o[:, :, units:] = give.astype(half).reshape(half_shape)
     first.step(2)
     second.step(1)
-    up_back.step(0)
-    down_back.step(0)
     first.step(3)
     second.step(2)
     first.step(4)
@@ -815,57 +823,48 @@
     sums_o[1:2] = offsets
     out_weight.wait()
     low = low_o[...].reshape(-1, width)
-    heads = term_vm.shape[2]
+    heads = term_vm.shape[0] // blocks
     for j in range(blocks):
         back = product(low, w_out[j].reshape(width, -1), NN).astype(half)
         mixed_vm[j] = back
         both = mixed[j] * back.astype(f32)
         owner = lax.broadcasted_iota(jnp.int32, both.shape, 1)
-        place_of = lax.broadcasted_iota(jnp.int32, (both.shape[0], heads), 1)
-        terms = jnp.zeros((both.shape[0], heads), f32)
         for h in range(heads):
             mine = (owner >= h * HEAD_DIM) & (owner < (h + 1) * HEAD_DIM)
             term = jnp.sum(jnp.where(mine, both, 0.0), axis=1, keepdims=True)
-            terms = jnp.where(place_of == h, term, terms)
-        term_vm[j] = terms
+            term_vm[j * heads + h : j * heads + h + 1] = as_row(term)
     back_swap.step(0)
     term_swap.step(0)
     second.step(3)
     second.step(4)
-    for part in (gather, first, second, up_back, down_back, back_swap, term_swap):
+    for part in parts:
         part.finish()
 
 
-def feed(place, own_rows, up_pieces, down_pieces, back_rows, after_attn, cot, mixed, norms, weights):
+def feed(place, own_rows, pieces, back_rows, after_attn, cot, mixed, norms, weights):
     half, f32 = jnp.bfloat16, jnp.float32
     gather = Gather(place, own_rows)
     rows = gather.out
     width = norms.shape[1]
     blocks, flat, block = mixed.shape
     heads = block // HEAD_DIM
-    units = up_pieces.shape[2]
+    units = pieces.shape[2] // 2
     per = math.prod(rows.shape[2:7])
     mixed_back = jax.ShapeDtypeStruct(mixed.shape, half)
-    terms = jax.ShapeDtypeStruct((blocks, flat, heads), f32)
+    terms = jax.ShapeDtypeStruct((blocks * heads, flat), f32)
     parts = [
         gather,
-        Swap(place, "dp", True, up_pieces),
-        Swap(place, "dp", True, down_pieces),
         Reduce(place, rows),
         Reduce(place, rows),
-        Swap(place, "dp", True, up_pieces),
-        Swap(place, "dp", True, down_pieces),
         Swap(place, "mp", False, mixed_back),
         Swap(place, "mp", False, terms),
     ]
     scratch = [
         pltpu.VMEM(rows.shape, half),
-        pltpu.VMEM(up_pieces.shape, half),
-        pltpu.VMEM(down_pieces.shape, half),
+        pltpu.VMEM((width, units), half),
+        pltpu.VMEM((width, units), half),
         pltpu.VMEM(rows.shape, half),
         pltpu.VMEM(rows.shape, half),
-        pltpu.VMEM(up_pieces.shape, half),
-        pltpu.VMEM(down_pieces.shape, half),
         pltpu.VMEM(weights.shape[:1] + weights.shape[2:], half),
         pltpu.VMEM((blocks, per, units), half),
         pltpu.VMEM((blocks, per, units), half),
@@ -879,10 +878,11 @@
     hbm = pl.BlockSpec(memory_space=pl.ANY)
     return pl.pallas_call(
         functools.partial(feed_kernel, place, parts),
-        in_specs=[hbm, hbm, hbm] + [whole] * 5 + [hbm],
-        out_specs=[hbm] * 6 + [whole] * 3,
-        out_shape=[part.out for part in parts[3:]]
+        in_specs=[hbm] + [whole] * 6 + [hbm],
+        out_specs=[hbm] * 4 + [whole] * 4,
+        out_shape=[part.out for part in parts[1:]]
         + [
+            jax.ShapeDtypeStruct(pieces.shape, half),
             jax.ShapeDtypeStruct(after_attn.shape, f32),
             jax.ShapeDtypeStruct(after_attn.shape, half),
             jax.ShapeDtypeStruct((2, width), f32),
@@ -892,24 +892,18 @@
             collective_id=3, has_side_effects=True, vmem_limit_bytes=60 * 1024 * 1024
         ),
         name="feed",
-    )(own_rows, up_pieces, down_pieces, back_rows, after_attn, cot, mixed, norms, weights)
-
-
-def feed_apart(place, own_rows, up_pieces, down_pieces, back_rows, after_attn, cot, mixed, norms, weights):
+    )(own_rows, pieces, back_rows, after_attn, cot, mixed, norms, weights)
+
+
+def feed_apart(place, own_rows, pieces, back_rows, after_attn, cot, mixed, norms, weights):
     half, f32 = jnp.bfloat16, jnp.float32
-    width, units = norms.shape[1], up_pieces.shape[2]
+    width, units = norms.shape[1], pieces.shape[2] // 2
     dot = functools.partial(jnp.einsum, preferred_element_type=f32)
-    ffn_rows, up_pieces, down_pieces = communicate(
-        "rows",
-        3,
-        [
-            Gather(place, own_rows),
-            Swap(place, "dp", True, up_pieces, 1),
-            Swap(place, "dp", True, down_pieces, 1),
-        ],
-    )
-    shape, pieces_shape = ffn_rows.shape, up_pieces.shape
-    w_up, w_down = up_pieces.reshape(width, units), down_pieces.reshape(width, units)
+    (ffn_rows,) = communicate("rows", 3, [Gather(place, own_rows)])
+    shape, half_shape = ffn_rows.shape, pieces.shape[:2] + (units,)
+    w_up, w_down = (
+        part.reshape(width, units) for part in (pieces[:, :, :units], pieces[:, :, units:])
+    )
     ffn_rows, back_rows = ffn_rows.reshape(-1, width), back_rows.reshape(-1, width)
     pre_act = dot("rd,df->rf", ffn_rows, w_up)
     hidden = exact_gelu(pre_act).astype(half)
@@ -919,15 +913,10 @@
     ffn_part = dot("rf,df->rd", hidden, w_down).astype(half)
     down_part = dot("rd,rf->df", back_rows, hidden).astype(half)
     up_part = dot("rd,rf->df", ffn_rows, pre_back).astype(half)
-    norm_pulled, ffn_out, up_owned, down_owned = communicate(
+    norm_pulled, ffn_out = communicate(
         "ffn",
         4,
-        [
-            Reduce(place, norm_part.reshape(shape)),
-            Reduce(place, ffn_part.reshape(shape)),
-            Swap(place, "dp", True, up_part.reshape(pieces_shape), 1),
-            Swap(place, "dp", True, down_part.reshape(pieces_shape), 1),
-        ],
+        [Reduce(place, norm_part.reshape(shape)), Reduce(place, ffn_part.reshape(shape))],
     )
     pull = jax.vjp(layer_norm, after_attn, norms[4], norms[5])[1]
     through, factor, offset = pull(norm_pulled.reshape(after_attn.shape))
@@ -937,6 +926,7 @@
     terms = jnp.sum(
         (mixed * mixed_back.astype(f32)).reshape(*mixed.shape[:2], -1, HEAD_DIM), axis=-1
     )
+    terms = terms.transpose(0, 2, 1).reshape(-1, mixed.shape[1])
     mixed_rows, terms = communicate(
         "back", 5, [Swap(place, "mp", False, mixed_back), Swap(place, "mp", False, terms)]
     )
@@ -944,23 +934,24 @@
     return (
         norm_pulled,
         ffn_out,
-        up_owned,
-        down_owned,
         mixed_rows,
         terms,
+        jnp.concatenate([up_part.reshape(half_shape), down_part.reshape(half_shape)], axis=2),
         after_back,
         low,
         sums,
     )
 
 
-def attend_back_kernel(place, heads, scale, reduce, latent_swap, totals, *refs):
+def attend_back_kernel(place, heads, scale, reduce, swap, latent_swap, totals, *refs):
     half, f32 = jnp.bfloat16, jnp.float32
-    (src, lat, q, p, blend, back, mix, low, row, wq, wk, wv, up_vm, down_vm) = refs[:14]
-    (media, time_rows, norms, latents, after_back, ffn_sums) = refs[14:20]
-    (grad_o, media_o, owned_o, latents_o, small_o, square_o) = refs[20:26]
-    (acc, lat_acc, lat_vm, kept, stage_a, stage_b, small, square, stage_sem) = refs[26:35]
-    rest = list(refs[35:])
+    (src, lat, q, p, blend, back, mix, low, row, wq, wk, wv, give) = refs[:13]
+    (media, time_rows, norms, latents, after_back, ffn_sums) = refs[13:19]
+    (grad_o, media_o, owned_o, ffn_o, latents_o, small_o, square_o) = refs[19:26]
+    (acc, lat_acc, lat_vm, kept, stage_a, stage_b, small, square, ffn_vm, joined, stage_sem) = refs[
+        26:37
+    ]
+    rest = list(refs[37:])
     phase, block = pl.program_id(0), pl.program_id(1)
     blocks = pl.num_programs(1)
     items = src.shape[0]
@@ -968,6 +959,7 @@
     width = src.shape[2]
     for part, give, out in (
         (reduce, grad_o, owned_o),
+        (swap, give, ffn_vm),
         (latent_swap, lat_acc, lat_vm),
         (totals[0], small, small_o),
         (totals[1], square, square_o),
@@ -1006,7 +998,11 @@
     def column(item, which):
         return as_column(row[0, item, which : which + 1])
 
-    at(0, 0, lambda: greet(latent_swap.peers() + reduce.peers()))
+    def start():
+        greet(swap.peers() + latent_swap.peers() + reduce.peers())
+        swap.step(0)
+
+    at(0, 0, start)
 
     @pl.when(phase == 0)
     def _():
@@ -1037,39 +1033,40 @@
 
     @pl.when(phase == 1)
     def _():
-        turns, queries, query_backs = [], [], []
+        turns = []
+        queries = jnp.concatenate([spread_heads(q[0, n], heads) for n in range(items)], axis=0)
+        back_s = jnp.concatenate([spread_heads(back[0, n], heads) for n in range(items)], axis=0)
+        pulls = product(back_s, wv[0, 0], NT).astype(half)
+        rows = pulls.shape[0] // items
         for n in range(items):
-            back_s = spread_heads(back[0, n], heads)
-            pull = product(back_s, wv[0, 0], NT).astype(half)
-            prob_back = product(pull, src[n], NT)
+            prob_back = product(pulls[n * rows : (n + 1) * rows], src[n], NT)
             score_back = (
                 p[0, n].astype(jnp.float32) * (column(n, 0) * scale) * (prob_back - column(n, 1))
             ).astype(half)
             kept[block, n] = score_back
-            turn = product(score_back, src[n], NN).astype(half)
-            query_back = fold_heads(product(turn, wk[0, 0], NN), heads).astype(half)
-            latent_back = product(query_back, wq[0, 0], NT)
-            latent_back = latent_back.reshape(lat_acc.shape[0], -1, width)
-
-            @pl.when(block == 0)
-            def _():
-                lat_acc[:, n] = latent_back
-
-            @pl.when(block > 0)
-            def _():
-                lat_acc[:, n] += latent_back
-
-            turns.append(turn)
-            queries.append(spread_heads(q[0, n], heads))
-            query_backs.append(query_back)
+            turns.append(product(score_back, src[n], NN).astype(half))
             if n + 1 < items:
                 events(1, n)
-        key_grad = product(
-            jnp.concatenate(turns, axis=0), jnp.concatenate(queries, axis=0), TN
-        )
-        query_grad = product(
-            lat[...].reshape(items * lat_total, width), jnp.concatenate(query_backs, axis=0), TN
-        )
+        turns = jnp.concatenate(turns, axis=0)
+        key_turns = product(turns, wk[0, 0], NN)
+        query_backs = jnp.concatenate(
+            [fold_heads(key_turns[n * rows : (n + 1) * rows], heads) for n in range(items)], axis=0
+        ).astype(half)
+        latent_back = product(query_backs, wq[0, 0], NT)
+        latent_back = latent_back.reshape(items, lat_acc.shape[0], -1, width)
+
+        @pl.when(block == 0)
+        def _():
+            for n in range(items):
+                lat_acc[:, n] = latent_back[n]
+
+        @pl.when(block > 0)
+        def _():
+            for n in range(items):
+                lat_acc[:, n] += latent_back[n]
+
+        key_grad = product(turns, queries, TN)
+        query_grad = product(lat[...].reshape(items * lat_total, width), query_backs, TN)
         hand_over(1, key_grad, 0, query_grad)
 
     events(1, items - 1)
@@ -1077,12 +1074,16 @@
 
     @pl.when(phase == 2)
     def _():
+        queries = jnp.concatenate([spread_heads(q[0, n], heads) for n in range(items)], axis=0)
+        back_s = jnp.concatenate([spread_heads(back[0, n], heads) for n in range(items)], axis=0)
+        pulls = product(back_s, wv[0, 0], NT)
+        reach = product(queries, wk[0, 0], NT).astype(half)
+        rows = pulls.shape[0] // items
         for n in range(items):
-            pull = product(spread_heads(back[0, n], heads), wv[0, 0], NT)
-            reach = product(spread_heads(q[0, n], heads), wk[0, 0], NT)
+            mine = slice(n * rows, (n + 1) * rows)
             value = product(
                 jnp.concatenate([kept[block, n], p[0, n]], axis=0),
-                jnp.concatenate([reach.astype(half), (pull * column(n, 0)).astype(half)], axis=0),
+                jnp.concatenate([reach[mine], (pulls[mine] * column(n, 0)).astype(half)], axis=0),
                 TN,
             )
 
@@ -1144,11 +1145,17 @@
         for move in moves_2[1:-1]:
             reduce.advance(*move)
         totals[0].advance(3)
+        swap.finish()
+        units = ffn_vm.shape[2] // 2
         sums = jnp.zeros((1, 1), f32)
-        for buffer in (up_vm, down_vm):
-            for k in range(buffer.shape[0]):
-                value = buffer[k].astype(f32)
-                sums = sums + jnp.sum(value * value, keepdims=True)
+        for k in range(ffn_vm.shape[0]):
+            piece = ffn_vm[k]
+            joined[0, :, k * units : (k + 1) * units] = piece[:, :units]
+            joined[1, :, k * units : (k + 1) * units] = piece[:, units:]
+            value = piece.astype(f32)
+            sums = sums + jnp.sum(value * value, keepdims=True)
+        ffn_out = pltpu.make_async_copy(joined, ffn_o, stage_sem.at[1])
+        ffn_out.start()
         reduce.advance(*moves_2[-1])
         totals[0].advance(4)
         owned = reduce.scr[reduce.out_spot]
@@ -1161,6 +1168,7 @@
         reduce.finish()
         for stage in range(1, 5):
             totals[1].advance(stage)
+        ffn_out.wait()
         out.wait()
 
     at(2, last, end)
@@ -1178,7 +1186,7 @@
     low,
     rows_in,
     weights,
-    owned_ffn,
+    give,
     rows_end,
     weight_halves,
     heads,
@@ -1199,6 +1207,8 @@
     reduce = Reduce(place, grad, kept=6 if weight_halves == 2 else 2)
     reduce.chunks = [(t, h) for t in order for h in range(weight_halves)]
     latent_swap = Swap(place, "mp", True, lat_shares)
+    swap = Swap(place, "dp", True, give)
+    joined = jax.ShapeDtypeStruct((2, give.shape[1], give.shape[0] * give.shape[2] // 2), half)
     small = jax.ShapeDtypeStruct((16, width), f32)
     square = jax.ShapeDtypeStruct((8, 128), f32)
     totals = [Total(place, small), Total(place, square)]
@@ -1235,13 +1245,15 @@
         pltpu.VMEM(inner, half),
         pltpu.VMEM(small.shape, f32),
         pltpu.VMEM(square.shape, f32),
+        pltpu.VMEM(give.shape, half),
+        pltpu.VMEM(joined.shape, half),
         pltpu.SemaphoreType.DMA((2,)),
     ]
-    for member in [reduce, latent_swap] + totals:
+    for member in [reduce, swap, latent_swap] + totals:
         scratch += member.scratch
     return pl.pallas_call(
         functools.partial(
-            attend_back_kernel, place, heads, scale, reduce, latent_swap, totals
+            attend_back_kernel, place, heads, scale, reduce, swap, latent_swap, totals
         ),
         grid=(3, blocks),
         in_specs=[
@@ -1257,13 +1269,15 @@
             weight(0, 1),
             weight(1, 1),
             weight(2, 1),
+            hbm,
         ]
-        + [whole] * 8,
-        out_specs=[hbm] * 3 + [whole] * 3,
+        + [whole] * 6,
+        out_specs=[hbm] * 4 + [whole] * 3,
         out_shape=[
             grad,
             jax.ShapeDtypeStruct((items, slots, width), f32),
             reduce.out,
+            joined,
             jax.ShapeDtypeStruct((items, own, width), f32),
             small,
             square,
@@ -1286,7 +1300,7 @@
         weights,
         weights,
         weights,
-        *owned_ffn,
+        give,
         *rows_end,
     )
 
@@ -1295,12 +1309,11 @@
     points = blocks * items
     if chunks == 8:
         eighths = {
-            (1, 0): [(0, 1), (1, 0)],
-            (1, 3): [(0, 2), (1, 1)],
-            (1, 6): [(0, 3), (1, 2)],
-            (1, 7): [(2, 0)],
-            (2, 0): [(2, 1), (1, 3)],
-            (2, 2): [(0, 4), (3, 0)],
+            (1, 1): [(0, 1), (1, 0)],
+            (1, 4): [(0, 2), (1, 1)],
+            (1, 7): [(2, 0), (0, 3), (1, 2)],
+            (2, 0): [(2, 1)],
+            (2, 3): [(0, 4), (3, 0), (1, 3)],
             (2, 4): [(3, 1)],
             (2, 6): [(2, 2)],
         }
@@ -1320,61 +1333,82 @@
     return plan, ((1, 2),), ((1, 3), (1, 4))
 
 
-def refresh_kernel(rates, *refs):
+def refresh_kernel(*refs):
     f32 = jnp.float32
-    count = len(rates)
-    square, small = refs[:2]
-    ins, outs = refs[2 : 2 + 4 * count], refs[2 + 4 * count :]
+    square, small, owned, ffn, media_in = refs[:5]
+    groups = [refs[5 + 3 * n : 8 + 3 * n] for n in range(6)]
+    norm_o, media_o = refs[23:25]
+    outs = [refs[25 + 5 * n : 30 + 5 * n] for n in range(4)]
+    outs += [refs[45 + 4 * n : 49 + 4 * n] for n in range(2)]
+    media_come = pltpu.make_async_copy(media_in, refs[53], refs[54].at[0])
+    media_come.start()
     total = square[0:1, 0:1] + jnp.sum(small[...] * small[...], keepdims=True)
     norm = jnp.sqrt(total)
-    outs[0][...] = norm
+    norm_o[...] = norm
     clip = 1.0 / jnp.maximum(norm, 1.0)
-    spot = 1
-    for n, rate in enumerate(rates):
-        grad, master, momentum, average = ins[4 * n : 4 * n + 4]
-        with_copy = n < 4
-        into = outs[spot : spot + (5 if with_copy else 4)]
-        spot += len(into)
-        rows = grad.shape[0]
-        step = math.gcd(rows, 32)
-
-        def update(at):
-            done = advance(
-                grad[at].astype(f32), master[at], momentum[at], average[at], clip, rate
-            )
-            for ref, value in zip(into, done):
-                ref[at] = value
-            if with_copy:
-                into[4][at] = done[1].astype(jnp.bfloat16)
-
-        if step < 16:
-            update(Ellipsis)
-        else:
-
-            def one(k, carry):
-                update(pl.ds(pl.multiple_of(k * step, step), step))
-                return carry
-
-            lax.fori_loop(0, rows // step, one, 0)
-
-
-def refresh(square, small, groups):
+
+    def update(number, at, gradient):
+        master, momentum, average = groups[number]
+        done = advance(
+            gradient.astype(f32),
+            master[at],
+            momentum[at],
+            average[at],
+            clip,
+            STEP_RATES[number],
+        )
+        for ref, value in zip(outs[number], done):
+            ref[at] = value
+        if number < 4:
+            outs[number][4][at] = done[1].astype(jnp.bfloat16)
+
+    parts, rows = owned.shape[1:3]
+    for h in range(parts):
+        for t in range(3):
+            update(0, (t, pl.ds(h * rows, rows)), owned[t, h])
+        update(1, pl.ds(h * rows, rows), owned[3, h])
+    media_come.wait()
+    media_go = pltpu.make_async_copy(refs[53], media_o, refs[54].at[1])
+    media_go.start()
+    step = math.gcd(ffn.shape[1], 16)
+
+    def one(k, carry):
+        at = pl.ds(pl.multiple_of(k * step, step), step)
+        for n in range(2):
+            update(2 + n, at, ffn[n, at])
+        return carry
+
+    lax.fori_loop(0, ffn.shape[1] // step, one, 0)
+    update(4, Ellipsis, small[0:6])
+    update(5, Ellipsis, small[6 : 6 + FRAMES])
+    media_go.wait()
+
+
+def refresh(square, small, owned, ffn, media_grad, groups):
     f32 = jnp.float32
     whole = pl.BlockSpec(memory_space=pltpu.VMEM)
-    shapes = [jax.ShapeDtypeStruct((1, 1), f32)]
-    for n, (rate, grad, *_) in enumerate(groups):
-        shapes += [jax.ShapeDtypeStruct(grad.shape, f32)] * 4
+    hbm = pl.BlockSpec(memory_space=pl.ANY)
+    shapes = [
+        jax.ShapeDtypeStruct((1, 1), f32),
+        jax.ShapeDtypeStruct(media_grad.shape, f32),
+    ]
+    for n, group in enumerate(groups):
+        shapes += [jax.ShapeDtypeStruct(group[0].shape, f32)] * 4
         if n < 4:
-            shapes.append(jax.ShapeDtypeStruct(grad.shape, jnp.bfloat16))
-    arrays = [array for _, *four in groups for array in four]
+            shapes.append(jax.ShapeDtypeStruct(group[0].shape, jnp.bfloat16))
+    arrays = [array for group in groups for array in group]
     return pl.pallas_call(
-        functools.partial(refresh_kernel, [rate for rate, *_ in groups]),
-        in_specs=[whole] * (2 + len(arrays)),
-        out_specs=[whole] * len(shapes),
+        refresh_kernel,
+        in_specs=[whole] * 4 + [hbm] + [whole] * len(arrays),
+        out_specs=[whole, hbm] + [whole] * (len(shapes) - 2),
         out_shape=shapes,
+        scratch_shapes=[
+            pltpu.VMEM(media_grad.shape, f32),
+            pltpu.SemaphoreType.DMA((2,)),
+        ],
         compiler_params=pltpu.CompilerParams(vmem_limit_bytes=60 * 1024 * 1024),
         name="refresh",
-    )(square, small, *arrays)
+    )(square, small, owned, ffn, media_grad, *arrays)
 
 
 def halves(rows):
@@ -1429,19 +1463,12 @@
         return rows.reshape(t, 1, own_rows // t, width)
 
     weight_halves = halves(rows_d)
-    own_weights = jnp.concatenate(
-        [qkv_master.astype(half), out_master.astype(half).T[None]], axis=0
-    ).reshape(4, weight_halves, rows_d // weight_halves, block)
-    latent_norm = layer_norm(latents, norm_params[2], norm_params[3]).astype(half)
-
     def as_pieces(wide):
         return wide.reshape(rows_d, dp_count, units).transpose(1, 0, 2)
 
-    def from_pieces(pieces):
-        return pieces.transpose(1, 0, 2).reshape(rows_d, hidden_block)
-
-    up_pieces = as_pieces(up_master.astype(half))
-    down_pieces = as_pieces(down_master.T.astype(half))
+    ffn_pieces = jnp.concatenate(
+        [as_pieces(up_master.astype(half)), as_pieces(down_master.T.astype(half))], axis=2
+    )
     slot_ids = mp_rank * slots + jnp.arange(slots)
     frame_ids = slot_ids // PATCHES
     keep = jnp.concatenate(
@@ -1457,15 +1484,19 @@
         blends,
         mixed_blocks,
         stats,
+        ffn_pieces,
     ) = front(
         place,
-        own_weights,
-        as_chunks(cotangent.astype(half)),
-        latent_norm,
+        qkv_master,
+        out_master.T,
+        as_chunks(cotangent),
+        latents,
+        ffn_pieces,
         media,
         keep.astype(f32)[:, None],
         time_table,
         norm_params,
+        weight_halves,
         heads,
         scale_factor,
     )
@@ -1489,18 +1520,16 @@
     (
         _,
         ffn_out,
-        up_owned,
-        down_owned,
         mixed_back_rows,
         row_terms,
+        give,
         after_back,
         attn_low,
         ffn_sums,
     ) = (feed if 2 * all_rows * width <= ROWS_IN_VMEM else feed_apart)(
         place,
         as_chunks(ffn_norm),
-        up_pieces,
-        down_pieces,
+        ffn_pieces,
         back_rows,
         after_attn.reshape(by_chunk),
         cotangent.reshape(by_chunk),
@@ -1510,14 +1539,14 @@
     )
     latents_out = after_attn + ffn_out.reshape(latents.shape)
     after_back, attn_low = after_back.reshape(latents.shape), attn_low.reshape(latents.shape)
-    row_terms = row_terms.reshape(mp_count, mp_count, items, lat_own, heads)
-    row_terms = row_terms.transpose(1, 2, 4, 0, 3).reshape(mp_count, items, heads * lat_total)
+    row_terms = row_terms.reshape(mp_count, mp_count, heads, items, lat_own)
+    row_terms = row_terms.transpose(1, 3, 2, 0, 4).reshape(mp_count, items, heads * lat_total)
     back_j = (
         mixed_back_rows.reshape(mp_count, mp_count, items, lat_own, block)
         .transpose(1, 2, 0, 3, 4)
         .reshape(mp_count, items, lat_total, block)
     )
-    _, media_grad, owned, latents_grad, small, square = attend_back(
+    _, media_grad, owned, ffn_owned, latents_grad, small, square = attend_back(
         place,
         source,
         latent_rows,
@@ -1529,36 +1558,23 @@
         attn_low,
         jnp.stack([share, row_terms], axis=2),
         weights,
-        [up_owned, down_owned],
+        give,
         [media, time_table, norm_params, latents, after_back, ffn_sums],
         weight_halves,
         heads,
         scale_factor,
     )
-    owned = owned.reshape(4, rows_d, block)
-    qkv_shape = (3 * rows_d, block)
     groups = [
-        (
-            STEP_RATES[0],
-            owned[:3].reshape(qkv_shape),
-            qkv_master.reshape(qkv_shape),
-            qkv_momentum.reshape(qkv_shape),
-            qkv_average.reshape(qkv_shape),
-        ),
-        (STEP_RATES[1], owned[3], out_master.T, out_momentum.T, out_average.T),
-        (STEP_RATES[2], from_pieces(up_owned), up_master, up_momentum, up_average),
-        (
-            STEP_RATES[3],
-            from_pieces(down_owned),
-            down_master.T,
-            down_momentum.T,
-            down_average.T,
-        ),
-        (STEP_RATES[4], small[:6], norm_params, norm_momentum, norm_average),
-        (STEP_RATES[5], small[6:14], time_table, time_momentum, time_average),
+        (qkv_master, qkv_momentum, qkv_average),
+        (out_master.T, out_momentum.T, out_average.T),
+        (up_master, up_momentum, up_average),
+        (down_master.T, down_momentum.T, down_average.T),
+        (norm_params, norm_momentum, norm_average),
+        (time_table, time_momentum, time_average),
     ]
     (
         grad_norm,
+        media_grad,
         qkv_grad,
         qkv_new,
         qkv_momentum_new,
@@ -1587,17 +1603,13 @@
         time_new,
         time_momentum_new,
         time_average_new,
-    ) = refresh(square, small, groups)
+    ) = refresh(square, small, owned, ffn_owned, media_grad, groups)
     grad_norm = grad_norm.reshape(())
     out_grad, out_new, out_momentum_new, out_average_new, out_copy = (
         value.T for value in (out_grad, out_new, out_momentum_new, out_average_new, out_copy)
     )
     down_grad, down_new, down_momentum_new, down_average_new, down_copy = (
         value.T for value in (down_grad, down_new, down_momentum_new, down_average_new, down_copy)
-    )
-    qkv_grad, qkv_new, qkv_momentum_new, qkv_average_new, qkv_copy = (
-        value.reshape(qkv_master.shape)
-        for value in (qkv_grad, qkv_new, qkv_momentum_new, qkv_average_new, qkv_copy)
     )
     return (
         latents_out,

time: 475 us -> 425 us (0.89)
  Pallas kernels: 427 us -> 400 us
  local copies, waits for them, and re-layouts: 31.3 us -> 12.2 us
    pallas_call x1, Pallas kernels: 131 us -> 88.5 us  [feed(): pl.pallas_call(functools.partial(feed_kernel, place, parts), in_specs=[hb...]
    pallas_call x1, Pallas kernels: 129 us -> 142 us  [front(): pl.pallas_call(functools.partial(front_kernel, place, heads, scale, halve...]
    unnamed x34 -> x23, local copies, waits for them, and re-layouts: 9.2 us -> 2.12 us
    slice x4 -> x0, local copies, waits for them, and re-layouts: 6.85 us -> none  [the longest x1 2.13 us: shards(): owned[:3].reshape(qkv_shape)]
where the time goes in v2:
time: 425 us; the launch traced here: 424 us
  Pallas kernels  400 us (94%)
  local copies, waits for them, and re-layouts  12.2 us (3%)
  other arithmetic  7.32 us (2%)
    pallas_call x1, Pallas kernels, attend_back(): pl.pallas_call(functools.partial(attend_back_kernel, place, heads, scale,...  154 us
    pallas_call x1, Pallas kernels, front(): pl.pallas_call(functools.partial(front_kernel, place, heads, scale, halve...  142 us
    pallas_call x1, Pallas kernels, feed(): pl.pallas_call(functools.partial(feed_kernel, place, parts), in_specs=[hb...  88.5 us
    pallas_call x1, Pallas kernels, refresh(): pl.pallas_call(refresh_kernel, in_specs=[whole] * 4 + [hbm] + [whole] * l...  16.1 us

profile of v2, /device:TPU:0, one launch (start us, length us, event | category | flops | bytes accessed | tf_op | source)
XLA Modules:
  0.0 424.3 jit_solution(2264012329435196402)
XLA Ops:
  0.7 0.7 broadcast_compare_fusion
  1.4 0.6 reshape.159.refs_6_
  2.0 1.5 slice_reduce_fusion.1
  3.5 1.4 convert_element_type.13
  5.0 0.6 reshape.147
  5.7 0.6 reshape.148
  6.3 0.3 copy_bitcast_fusion
  6.6 1.5 pad_maximum_fusion.refs_4_
  8.1 141.6 %front.1 = (bf16[2,2,4,4,2,2,96,384]{7,6,5,4,3,2,1,0:T(8,128)(2,1)}, bf16[2,2,2,4,2,1,16,1536]{7,6,5,4,3,2,1,0:T(8,128)(2,1)}, bf16[2,528,1536]{2,1,0:T(8,128)(2...) custom-call(f32[3,192,384]{2,1,0:T(8,128)} %refs_5_.3, ...), custom_call_target="tpu_custom_call" | custom-call | tf_op jit(solution)/shard_map/front/pallas_call | solution.py:721
  149.7 0.9 slice.16
  150.6 0.9 copy.64
  152.0 0.1 squeeze.13
  152.1 0.1 fusion.6
  152.2 0.3 copy.65
  152.5 0.8 copy.68
  153.2 0.6 broadcast_in_dim.8
  153.9 0.5 reshape.149
  154.4 0.6 copy-done.5
  155.0 0.1 multiply_reduce_fusion
  155.1 0.8 copy-done.3
  155.9 4.0 fusion.13
  159.9 0.2 multiply_reduce_fusion.1
  160.1 0.7 fusion.3.refs_0_
  160.9 88.5 %feed.1 = (f32[2,1,16,1536]{3,2,1,0:T(8,128)}, f32[2,1,16,1536]{3,2,1,0:T(8,128)}, bf16[4,4,32,384]{3,2,1,0:T(8,128)(2,1)}, f32[4,16,32]{2,1,0:T(8,128)}, bf16[8...) custom-call(bf16[2,1,16,1536]{3,2,1,0:T(8,128)(2,1)} %fusion.3.refs_0_, ...), custom_call_target="tpu_custom_call" | custom-call | tf_op jit(solution)/shard_map/feed/pallas_call | solution.py:879
  249.4 1.7 bitcast_add_fusion
  251.1 1.8 copy.69
  252.9 0.1 reshape.157
  253.0 0.1 stack_reshape.3
  253.2 0.6 pad_maximum_fusion.1.refs_8_
  253.8 153.7 %attend_back.1 = (bf16[2,2,4,4,2,2,96,384]{7,6,5,4,3,2,1,0:T(8,128)(2,1)}, f32[2,512,1536]{2,1,0:T(8,128)}, f32[4,2,96,384]{3,2,1,0:T(8,128)}, bf16[2,192,1536]{...) custom-call(bf16[2,528,1536]{2,1,0:T(8,128)(2,1)} %get-tuple-element.91.refs_0_, ...), custom_call_target="tpu_custom_call" | custom-call | tf_op jit(solution)/shard_map/attend_back/pallas_call | solution.py:1254
  407.5 16.1 %refresh.1 = (f32[1,1]{1,0:T(1,128)}, f32[2,512,1536]{2,1,0:T(8,128)}, f32[3,192,384]{2,1,0:T(8,128)}, f32[3,192,384]{2,1,0:T(8,128)}, f32[3,192,384]{2,1,0:T(8,...) custom-call(f32[8,128]{1,0:T(8,128)} %get-tuple-element.103.refs_0_,, ...), custom_call_target="tpu_custom_call" | custom-call | tf_op jit(solution)/shard_map/refresh/pallas_call | solution.py:1400
  423.6 0.7 copy.80
  (35 shorter events, 0.6 us)
Async XLA Ops:
  3.5 2.0 copy-start.1
  149.7 2.8 copy-start.6
  153.9 1.1 copy-start.5
  155.0 0.9 copy-start.3
  155.1 4.8 %copy-start.2 = (f32[4,2,16,384]{3,2,1,0:T(8,128)}, f32[4,2,16,384]{3,2,1,0:T(8,128)S(1)}, u32[]{:S(2)}) copy-start(f32[4,2,16,384]{3,2,1,0:T(8,128)S(1)} %multiply_reduce_fusion) | copy-start | bytes 589828
  155.9 4.0 copy-start.4
  155.9 4.2 copy-start.9
  155.9 4.2 copy-start.10
  159.9 1.0 copy-start
  249.4 3.5 copy-start.8
  407.5 16.1 %copy-start.7 = (f32[2,16,1536]{2,1,0:T(8,128)S(1)}, f32[2,16,1536]{2,1,0:T(8,128)}, u32[]{:S(2)}) copy-start(f32[2,16,1536]{2,1,0:T(8,128)} %get-tuple-element.181) | copy-start | bytes 589828

commit v3 on v2

--- a/solution.py
+++ b/solution.py
@@ -288,8 +288,7 @@
     def part(self, n, stage, at):
         order = BACK_ORDERS[n % 2]
         if stage == 0:
-            t, h = self.chunks[n]
-            return self.src.at[:, at, t, :, :, h]
+            return self.source(n, at)
         index = tuple(
             at if a == order[stage] else self.me[a] if a in order[:stage] else slice(None)
             for a in LAYOUT
@@ -313,16 +312,22 @@
                 self.place.device(there),
             )
 
+    def source(self, n, at):
+        t, h = self.chunks[n]
+        if t in self.apart:
+            return self.apart[t].at[:, at, :, :, h]
+        return self.src.at[:, at, t, :, :, h]
+
     def own(self, n):
-        t, h = self.chunks[n]
         return pltpu.make_async_copy(
-            self.src.at[:, self.me["c"], t, :, :, h],
+            self.source(n, self.me["c"]),
             self.scr[2].at[n % self.kept],
             self.scr[0].at[n, 4, 0],
         )
 
-    def begin(self, refs):
+    def begin(self, refs, apart=()):
         self.src, self.dst, self.scr = refs[0], refs[1], refs[2:]
+        self.apart = dict(apart)
         self.me = self.place.mine()
 
     def steps(self):
@@ -409,17 +414,27 @@
 
 
 class Total:
-    AXES = ("c", "y", "x", "z")
-
-    def __init__(self, place, value):
-        self.place, self.value = place, value
+    def __init__(self, place, value, axes=("c", "y", "x", "z"), split=False):
+        self.place, self.value, self.split = place, value, split
+        self.axes = axes + ("c",) if split else axes
         self.out = jax.ShapeDtypeStruct(value.shape, value.dtype)
-        sems = pltpu.SemaphoreType.DMA((4, max(place.size.values())))
+        self.half = value.shape[0] // 2 if split else value.shape[0]
+        sizes = [self.size(a) for a in self.axes]
+        sems = pltpu.SemaphoreType.DMA((len(sizes), max(sizes)))
         self.scratch = [sems, sems] + [
-            pltpu.VMEM((place.size[a],) + value.shape, value.dtype) for a in self.AXES
+            pltpu.VMEM(
+                (size, self.half if k else value.shape[0]) + value.shape[1:], value.dtype
+            )
+            for k, size in enumerate(sizes)
         ]
 
     peers = Gather.peers
+
+    def size(self, axis):
+        return self.place.count[axis] if axis in self.place.count else self.place.size[axis]
+
+    def spot(self, axis):
+        return lax.axis_index(axis) if axis in self.place.count else self.me[axis]
 
     def begin(self, refs):
         self.src, self.dst, self.send, self.recv = refs[:4]
@@ -427,18 +442,22 @@
         self.me = self.place.mine()
 
     def copies(self, stage, receive):
-        axis = self.AXES[stage]
-        size = self.place.size[axis]
-        buf, me = self.bufs[stage], self.me
+        axis = self.axes[stage]
+        size = self.size(axis)
+        buf, mine = self.bufs[stage], self.spot(axis)
         for k in range(1, size):
-            there = self.place.shifted(me, axis, k)
-            here = self.place.shifted(me, axis, size - k)
+            there = lax.rem(mine + k, size)
+            here = lax.rem(mine + size - k, size)
+            if axis in self.place.count:
+                device = {axis: there}
+            else:
+                device = self.place.device({**self.me, axis: there})
             yield remote(
-                buf.at[me[axis]],
-                buf.at[here[axis] if receive else me[axis]],
+                buf.at[mine],
+                buf.at[here if receive else mine],
                 self.send.at[stage, k],
                 self.recv.at[stage, k],
-                self.place.device(there),
+                device,
             )
 
     def advance(self, stage):
@@ -449,13 +468,22 @@
                 copy.wait_recv()
             for copy in self.copies(stage - 1, False):
                 copy.wait_send()
-            value = self.bufs[stage - 1][0]
-            for k in range(1, self.place.size[self.AXES[stage - 1]]):
-                value = value + self.bufs[stage - 1][k]
-        if stage == 4:
+            buf, size = self.bufs[stage - 1], self.size(self.axes[stage - 1])
+            if self.split and stage == len(self.axes):
+                for k in range(size):
+                    self.dst[k * self.half : (k + 1) * self.half] = buf[k]
+                return
+            if self.split and stage == 1:
+                rows = pl.ds(pl.multiple_of(self.me["c"] * self.half, self.half), self.half)
+            else:
+                rows = slice(None)
+            value = buf[0, rows]
+            for k in range(1, size):
+                value = value + buf[k, rows]
+        if stage == len(self.axes):
             self.dst[...] = value
             return
-        self.bufs[stage][self.me[self.AXES[stage]]] = value
+        self.bufs[stage][self.spot(self.axes[stage])] = value
         for copy in self.copies(stage, False):
             copy.start()
 
@@ -554,15 +582,15 @@
     qkv, out_t, cot_in, latents, ffn_in, media, keep, time_rows, norms = refs[:9]
     w_o, back_o, src_o, lat_o, q_o, p_o, blend_o, mixed_o, stat_o, ffn_o = refs[9:19]
     w_vm, lat_vm, src_vm, q_vm, p_vm, blend_vm, mixed_vm, stat_vm, sems = refs[19:28]
-    own_w, cot, lat_in = refs[28:31]
-    rest = list(refs[31:])
+    own_w, cot, lat_in, stat_all = refs[28:32]
+    rest = list(refs[32:])
     gather_w, gather_c, lat_swap, mixed_swap, stat_swap, ffn_swap = parts
     ends = (
         (own_w, w_vm),
         (cot, back_o),
         (lat_in, lat_vm),
         (mixed_vm, mixed_o),
-        (stat_vm, stat_o),
+        (stat_vm, stat_all),
         (ffn_in, ffn_o),
     )
     for part, end in zip(parts, ends):
@@ -673,6 +701,12 @@
     for part in parts:
         if part is not lat_swap:
             part.finish()
+    peaks = [stat_all[k, :, :, 0] for k in range(blocks)]
+    top = functools.reduce(jnp.maximum, peaks)
+    grow = [jnp.exp(peak - top) for peak in peaks]
+    total = sum(stat_all[k, :, :, 1] * grow[k] for k in range(blocks))
+    for k in range(blocks):
+        stat_o[k] = grow[k] / total
     for copy in kept:
         copy.wait()
 
@@ -714,6 +748,7 @@
     scratch = [pltpu.VMEM(shape.shape, shape.dtype) for shape in shapes]
     scratch.append(pltpu.SemaphoreType.DMA((8,)))
     scratch += [pltpu.VMEM(v.shape, half) for v in (own_weights, low_cot, latent_norm)]
+    scratch.append(pltpu.VMEM(parts[4].out.shape, f32))
     for part in parts:
         scratch += part.scratch
     whole = pl.BlockSpec(memory_space=pltpu.VMEM)
@@ -721,7 +756,7 @@
     return pl.pallas_call(
         functools.partial(front_kernel, place, heads, scale, halves_w, parts),
         in_specs=[whole] * 4 + [hbm] + [whole] * 4,
-        out_specs=[hbm] * 10,
+        out_specs=[hbm] * 8 + [whole, hbm],
         out_shape=[
             parts[0].out,
             parts[1].out,
@@ -731,7 +766,7 @@
             shapes[4],
             shapes[5],
             parts[3].out,
-            parts[4].out,
+            jax.ShapeDtypeStruct((blocks, blocks, items, rows), f32),
             parts[5].out,
         ],
         scratch_shapes=scratch,
@@ -742,13 +777,18 @@
     )(qkv, out_t, cot, latents, ffn_pieces, media, keep, time_rows, norms)
 
 
+def out_grad_shape(place, width, halves_w, block):
+    s = place.size
+    return (s["y"], s["c"], s["z"], s["x"], halves_w, width // (s["z"] * s["x"] * halves_w), block)
+
+
 def feed_kernel(place, parts, *refs):
     half, f32 = jnp.bfloat16, jnp.float32
     own_rows, pieces, back_rows, after_attn, cot, mixed, norms, weights = refs[:8]
-    (norm_o, ffn_o, back_o, term_o, give_o, after_o, low_o, sums_o) = refs[8:16]
-    (rows_vm, up_vm, down_vm, share_a, share_b, w_out) = refs[16:22]
-    (hid_vm, pre_vm, mixed_vm, term_vm, sem) = refs[22:27]
-    rest = list(refs[27:])
+    (norm_o, ffn_o, back_o, term_o, grad_o, give_o, after_o, low_o, sums_o, lat_o) = refs[8:18]
+    (rows_vm, up_vm, down_vm, share_a, share_b, w_out) = refs[18:24]
+    (hid_vm, pre_vm, mixed_vm, term_vm, grad_vm, sem) = refs[24:30]
+    rest = list(refs[30:])
     gather, first, second, back_swap, term_swap = parts
     ends = (
         (own_rows, rows_vm),
@@ -836,12 +876,22 @@
     back_swap.step(0)
     term_swap.step(0)
     second.step(3)
+    for j in range(blocks):
+        grad = product(low, mixed[j].astype(half), TN).astype(half)
+        grad_vm[j // c_count, j % c_count] = grad.reshape(grad_vm.shape[2:])
+    grad_copy = pltpu.make_async_copy(grad_vm, grad_o, sem.at[1])
+    grad_copy.start()
     second.step(4)
+    for t in range(after_attn.shape[0]):
+        lat_o[t] = after_attn[t] + second.scr[second.out_spot][t, 0]
     for part in parts:
         part.finish()
-
-
-def feed(place, own_rows, pieces, back_rows, after_attn, cot, mixed, norms, weights):
+    grad_copy.wait()
+
+
+def feed(
+    place, own_rows, pieces, back_rows, after_attn, cot, mixed, norms, weights, halves_w
+):
     half, f32 = jnp.bfloat16, jnp.float32
     gather = Gather(place, own_rows)
     rows = gather.out
@@ -852,6 +902,7 @@
     per = math.prod(rows.shape[2:7])
     mixed_back = jax.ShapeDtypeStruct(mixed.shape, half)
     terms = jax.ShapeDtypeStruct((blocks * heads, flat), f32)
+    grad = jax.ShapeDtypeStruct(out_grad_shape(place, width, halves_w, block), half)
     parts = [
         gather,
         Reduce(place, rows),
@@ -870,7 +921,8 @@
         pltpu.VMEM((blocks, per, units), half),
         pltpu.VMEM(mixed.shape, half),
         pltpu.VMEM(terms.shape, f32),
-        pltpu.SemaphoreType.DMA((1,)),
+        pltpu.VMEM(grad.shape, half),
+        pltpu.SemaphoreType.DMA((2,)),
     ]
     for part in parts:
         scratch += part.scratch
@@ -879,13 +931,15 @@
     return pl.pallas_call(
         functools.partial(feed_kernel, place, parts),
         in_specs=[hbm] + [whole] * 6 + [hbm],
-        out_specs=[hbm] * 4 + [whole] * 4,
+        out_specs=[hbm] * 5 + [whole] * 5,
         out_shape=[part.out for part in parts[1:]]
         + [
+            grad,
             jax.ShapeDtypeStruct(pieces.shape, half),
             jax.ShapeDtypeStruct(after_attn.shape, f32),
             jax.ShapeDtypeStruct(after_attn.shape, half),
             jax.ShapeDtypeStruct((2, width), f32),
+            jax.ShapeDtypeStruct(after_attn.shape, f32),
         ],
         scratch_shapes=scratch,
         compiler_params=pltpu.CompilerParams(
@@ -895,7 +949,9 @@
     )(own_rows, pieces, back_rows, after_attn, cot, mixed, norms, weights)
 
 
-def feed_apart(place, own_rows, pieces, back_rows, after_attn, cot, mixed, norms, weights):
+def feed_apart(
+    place, own_rows, pieces, back_rows, after_attn, cot, mixed, norms, weights, halves_w
+):
     half, f32 = jnp.bfloat16, jnp.float32
     width, units = norms.shape[1], pieces.shape[2] // 2
     dot = functools.partial(jnp.einsum, preferred_element_type=f32)
@@ -931,27 +987,30 @@
         "back", 5, [Swap(place, "mp", False, mixed_back), Swap(place, "mp", False, terms)]
     )
     sums = jnp.stack([factor, offset])
+    grad = dot("ld,jle->jde", low.reshape(-1, width), mixed.astype(half)).astype(half)
     return (
         norm_pulled,
         ffn_out,
         mixed_rows,
         terms,
+        grad.reshape(out_grad_shape(place, width, halves_w, mixed.shape[2])),
         jnp.concatenate([up_part.reshape(half_shape), down_part.reshape(half_shape)], axis=2),
         after_back,
         low,
         sums,
+        after_attn + ffn_out.reshape(after_attn.shape),
     )
 
 
 def attend_back_kernel(place, heads, scale, reduce, swap, latent_swap, totals, *refs):
     half, f32 = jnp.bfloat16, jnp.float32
-    (src, lat, q, p, blend, back, mix, low, row, wq, wk, wv, give) = refs[:13]
-    (media, time_rows, norms, latents, after_back, ffn_sums) = refs[13:19]
-    (grad_o, media_o, owned_o, ffn_o, latents_o, small_o, square_o) = refs[19:26]
+    (src, lat, q, p, blend, back, out_part, row, wq, wk, wv, give) = refs[:12]
+    (media, time_rows, norms, latents, after_back, ffn_sums) = refs[12:18]
+    (grad_o, media_o, owned_o, ffn_o, latents_o, small_o, square_o) = refs[18:25]
     (acc, lat_acc, lat_vm, kept, stage_a, stage_b, small, square, ffn_vm, joined, stage_sem) = refs[
-        26:37
+        25:36
     ]
-    rest = list(refs[37:])
+    rest = list(refs[36:])
     phase, block = pl.program_id(0), pl.program_id(1)
     blocks = pl.num_programs(1)
     items = src.shape[0]
@@ -965,7 +1024,10 @@
         (totals[1], square, square_o),
     ):
         size = len(part.scratch)
-        part.begin((give, out) + tuple(rest[:size]))
+        if part is reduce:
+            part.begin((give, out) + tuple(rest[:size]), {3: out_part})
+        else:
+            part.begin((give, out) + tuple(rest[:size]))
         rest = rest[size:]
 
     def at(number, index, action):
@@ -979,27 +1041,42 @@
     def staged(t, buffer, number):
         return pltpu.make_async_copy(buffer, grad_o.at[y_of, c_of, t], stage_sem.at[number])
 
-    def hand_over(first, first_value, second, second_value):
+    def hand_over(*shares):
         @pl.when(block > 0)
         def _():
-            staged(first, stage_a, 0).wait()
-            staged(second, stage_b, 1).wait()
-
-        stage_a[...] = first_value.astype(half).reshape(stage_a.shape)
-        stage_b[...] = second_value.astype(half).reshape(stage_b.shape)
-        staged(first, stage_a, 0).start()
-        staged(second, stage_b, 1).start()
+            for k, (t, _) in enumerate(shares):
+                staged(t, (stage_a, stage_b)[k], k).wait()
+
+        for k, (t, value) in enumerate(shares):
+            buffer = (stage_a, stage_b)[k]
+            buffer[...] = value.astype(half).reshape(buffer.shape)
+            staged(t, buffer, k).start()
 
         @pl.when(block == last)
         def _():
-            staged(first, stage_a, 0).wait()
-            staged(second, stage_b, 1).wait()
+            for k, (t, _) in enumerate(shares):
+                staged(t, (stage_a, stage_b)[k], k).wait()
+
+    def of_item(ref, item):
+        return ref[:, 0, item].reshape(lat_total, ref.shape[4])
 
     def column(item, which):
         return as_column(row[0, item, which : which + 1])
 
+    def events(number, half_step):
+        for (where, point), moves in plan.items():
+            if where == number and point % items == half_step:
+
+                def carry_out(moves=moves):
+                    for move in moves:
+                        reduce.advance(*move)
+
+                at(where, point // items, carry_out)
+
     def start():
         greet(swap.peers() + latent_swap.peers() + reduce.peers())
+        if len(reduce.chunks) == 8:
+            reduce.advance(0, 0)
         swap.step(0)
 
     at(0, 0, start)
@@ -1008,34 +1085,21 @@
     def _():
         back_s = jnp.concatenate(
             [
-                (spread_heads(back[0, n], heads) * column(n, 0)).astype(half)
+                (spread_heads(of_item(back, n), heads) * column(n, 0)).astype(half)
                 for n in range(items)
             ],
             axis=0,
         )
         value_grad = product(blend[0].reshape(back_s.shape[0], width), back_s, TN)
-        out_grad = product(
-            low[...].reshape(-1, width), mix[0].reshape(-1, mix.shape[3]), TN
-        )
-        hand_over(3, out_grad, 2, value_grad)
-
-    def events(number, half_step):
-        for (where, point), moves in plan.items():
-            if where == number and point % items == half_step:
-
-                def carry_out(moves=moves):
-                    for move in moves:
-                        reduce.advance(*move)
-
-                at(where, point // items, carry_out)
-
-    at(1, 0, lambda: reduce.advance(0, 0))
+        hand_over((2, value_grad))
+
+    events(0, items - 1)
 
     @pl.when(phase == 1)
     def _():
         turns = []
         queries = jnp.concatenate([spread_heads(q[0, n], heads) for n in range(items)], axis=0)
-        back_s = jnp.concatenate([spread_heads(back[0, n], heads) for n in range(items)], axis=0)
+        back_s = jnp.concatenate([spread_heads(of_item(back, n), heads) for n in range(items)], axis=0)
         pulls = product(back_s, wv[0, 0], NT).astype(half)
         rows = pulls.shape[0] // items
         for n in range(items):
@@ -1067,7 +1131,7 @@
 
         key_grad = product(turns, queries, TN)
         query_grad = product(lat[...].reshape(items * lat_total, width), query_backs, TN)
-        hand_over(1, key_grad, 0, query_grad)
+        hand_over((1, key_grad), (0, query_grad))
 
     events(1, items - 1)
     at(1, last, lambda: latent_swap.step(0))
@@ -1075,7 +1139,7 @@
     @pl.when(phase == 2)
     def _():
         queries = jnp.concatenate([spread_heads(q[0, n], heads) for n in range(items)], axis=0)
-        back_s = jnp.concatenate([spread_heads(back[0, n], heads) for n in range(items)], axis=0)
+        back_s = jnp.concatenate([spread_heads(of_item(back, n), heads) for n in range(items)], axis=0)
         pulls = product(back_s, wv[0, 0], NT)
         reach = product(queries, wk[0, 0], NT).astype(half)
         rows = pulls.shape[0] // items
@@ -1156,8 +1220,10 @@
             sums = sums + jnp.sum(value * value, keepdims=True)
         ffn_out = pltpu.make_async_copy(joined, ffn_o, stage_sem.at[1])
         ffn_out.start()
+        totals[0].advance(4)
         reduce.advance(*moves_2[-1])
-        totals[0].advance(4)
+        if totals[0].split:
+            totals[0].advance(5)
         owned = reduce.scr[reduce.out_spot]
         for t in range(owned.shape[0]):
             for h in range(owned.shape[1]):
@@ -1166,7 +1232,7 @@
         square[...] = jnp.broadcast_to(sums, square.shape)
         totals[1].advance(0)
         reduce.finish()
-        for stage in range(1, 5):
+        for stage in range(1, 3):
             totals[1].advance(stage)
         ffn_out.wait()
         out.wait()
@@ -1182,8 +1248,7 @@
     chance,
     blend,
     back,
-    mixed,
-    low,
+    out_part,
     rows_in,
     weights,
     give,
@@ -1194,7 +1259,7 @@
 ):
     items, keys, width = source.shape
     lat = latent_rows.shape[1]
-    own = low.shape[1]
+    own = back.shape[3]
     blocks, block = weights.shape[0], weights.shape[3]
     rows = heads * lat
     half, f32 = jnp.bfloat16, jnp.float32
@@ -1211,7 +1276,10 @@
     joined = jax.ShapeDtypeStruct((2, give.shape[1], give.shape[0] * give.shape[2] // 2), half)
     small = jax.ShapeDtypeStruct((16, width), f32)
     square = jax.ShapeDtypeStruct((8, 128), f32)
-    totals = [Total(place, small), Total(place, square)]
+    totals = [
+        Total(place, small, split=s["c"] == 2),
+        Total(place, square, axes=("mp", "dp")),
+    ]
     slots = keys - own
 
     def weight(t, first):
@@ -1262,9 +1330,10 @@
             late(lat, block),
             late(rows, keys),
             early(rows, width),
-            per(lat, block),
-            early(own, block),
-            whole,
+            pl.BlockSpec(
+                (blocks, 1, items, own, block), lambda ph, j: (0, j, 0, 0, 0)
+            ),
+            hbm,
             per(2, rows),
             weight(0, 1),
             weight(1, 1),
@@ -1294,8 +1363,7 @@
         chance,
         blend,
         back,
-        mixed,
-        low,
+        out_part,
         rows_in,
         weights,
         weights,
@@ -1309,28 +1377,31 @@
     points = blocks * items
     if chunks == 8:
         eighths = {
-            (1, 1): [(0, 1), (1, 0)],
-            (1, 4): [(0, 2), (1, 1)],
-            (1, 7): [(2, 0), (0, 3), (1, 2)],
-            (2, 0): [(2, 1)],
-            (2, 3): [(0, 4), (3, 0), (1, 3)],
+            (0, 1): [(0, 1)],
+            (0, 7): [(1, 0)],
+            (1, 2): [(0, 2), (1, 1)],
+            (1, 5): [(0, 3), (1, 2)],
+            (1, 7): [(2, 0)],
+            (2, 0): [(2, 1), (0, 4), (3, 0)],
+            (2, 3): [(1, 3)],
             (2, 4): [(3, 1)],
             (2, 6): [(2, 2)],
         }
+        ends = ((1, 4), (3, 2), (2, 3)), ((3, 3), (2, 4), (3, 4))
     else:
         eighths = {
-            (1, 0): [(0, 1)],
+            (0, 7): [(0, 0)],
+            (1, 1): [(0, 1)],
             (1, 3): [(0, 2)],
             (1, 6): [(0, 3)],
             (1, 7): [(0, 4), (1, 0)],
             (2, 0): [(1, 1)],
         }
+        ends = ((1, 2),), ((1, 3), (1, 4))
     plan = {
         (phase, (eighth + 1) * points // 8 - 1): moves for (phase, eighth), moves in eighths.items()
     }
-    if chunks == 8:
-        return plan, ((1, 4), (3, 2), (2, 3)), ((3, 3), (2, 4), (3, 4))
-    return plan, ((1, 2),), ((1, 3), (1, 4))
+    return plan, *ends
 
 
 def refresh_kernel(*refs):
@@ -1483,7 +1554,7 @@
         chances,
         blends,
         mixed_blocks,
-        stats,
+        shares,
         ffn_pieces,
     ) = front(
         place,
@@ -1503,9 +1574,6 @@
     weights = weights.reshape(mp_count, 4, width, block)
     w_out = weights[:, 3]
     latent_rows = latent_rows.transpose(1, 0, 2, 3).reshape(items, lat_total, width)
-    part_peaks, part_sums = stats[:, :, :, 0], stats[:, :, :, 1]
-    grow = jnp.exp(part_peaks - jnp.max(part_peaks, axis=0))
-    shares = grow / jnp.sum(part_sums * grow, axis=0)
     share = lax.dynamic_index_in_dim(shares, mp_rank, 0, keepdims=False)
     own_shares = lax.dynamic_slice_in_dim(
         shares.reshape(mp_count, mp_count, items, heads, lat_total), mp_rank * lat_own, lat_own, 4
@@ -1519,13 +1587,15 @@
     by_chunk = (t, own_rows // t, width)
     (
         _,
-        ffn_out,
+        _,
         mixed_back_rows,
         row_terms,
+        out_part,
         give,
         after_back,
         attn_low,
         ffn_sums,
+        latents_out,
     ) = (feed if 2 * all_rows * width <= ROWS_IN_VMEM else feed_apart)(
         place,
         as_chunks(ffn_norm),
@@ -1536,16 +1606,12 @@
         mixed_full.reshape(mp_count, own_rows, block),
         norm_params,
         weights,
-    )
-    latents_out = after_attn + ffn_out.reshape(latents.shape)
-    after_back, attn_low = after_back.reshape(latents.shape), attn_low.reshape(latents.shape)
+        weight_halves,
+    )
+    latents_out, after_back = latents_out.reshape(latents.shape), after_back.reshape(latents.shape)
     row_terms = row_terms.reshape(mp_count, mp_count, heads, items, lat_own)
     row_terms = row_terms.transpose(1, 3, 2, 0, 4).reshape(mp_count, items, heads * lat_total)
-    back_j = (
-        mixed_back_rows.reshape(mp_count, mp_count, items, lat_own, block)
-        .transpose(1, 2, 0, 3, 4)
-        .reshape(mp_count, items, lat_total, block)
-    )
+    back_j = mixed_back_rows.reshape(mp_count, mp_count, items, lat_own, block)
     _, media_grad, owned, ffn_owned, latents_grad, small, square = attend_back(
         place,
         source,
@@ -1554,8 +1620,7 @@
         chances,
         blends,
         back_j,
-        mixed_j,
-        attn_low,
+        out_part,
         jnp.stack([share, row_terms], axis=2),
         weights,
         give,

time: 425 us -> 417 us (0.981)
  Pallas kernels: 400 us -> 394 us
    pallas_call x1, Pallas kernels: 154 us -> 147 us  [attend_back(): pl.pallas_call(functools.partial(attend_back_kernel, place, heads, scale,...]
where the time goes in v3:
time: 417 us; the launch traced here: 416 us
  Pallas kernels  394 us (94%)
  local copies, waits for them, and re-layouts  12.3 us (3%)
  other arithmetic  5.37 us (1%)
    pallas_call x1, Pallas kernels, attend_back(): pl.pallas_call(functools.partial(attend_back_kernel, place, heads, scale,...  147 us
    pallas_call x1, Pallas kernels, front(): pl.pallas_call(functools.partial(front_kernel, place, heads, scale, halve...  142 us
    pallas_call x1, Pallas kernels, feed(): pl.pallas_call(functools.partial(feed_kernel, place, parts), in_specs=[hb...  88.6 us
    pallas_call x1, Pallas kernels, refresh(): pl.pallas_call(refresh_kernel, in_specs=[whole] * 4 + [hbm] + [whole] * l...  16.2 us

profile of v3, /device:TPU:0, one launch (start us, length us, event | category | flops | bytes accessed | tf_op | source)
XLA Modules:
  0.0 416.1 jit_solution(6414191152938780119)
XLA Ops:
  0.7 0.7 broadcast_compare_fusion
  1.4 0.6 reshape.147.refs_6_
  2.0 1.5 slice_reduce_fusion.1
  3.5 1.4 convert_element_type.13
  5.0 0.6 reshape.136
  5.6 0.1 bitcast_convert_fusion
  5.7 0.6 reshape.137
  6.3 0.3 copy_bitcast_fusion
  6.6 1.5 pad_maximum_fusion.refs_4_
  8.1 142.1 %front.1 = (bf16[2,2,4,4,2,2,96,384]{7,6,5,4,3,2,1,0:T(8,128)(2,1)}, bf16[2,2,2,4,2,1,16,1536]{7,6,5,4,3,2,1,0:T(8,128)(2,1)}, bf16[2,528,1536]{2,1,0:T(8,128)(2...) custom-call(f32[3,192,384]{2,1,0:T(8,128)} %refs_5_.3, ...), custom_call_target="tpu_custom_call" | custom-call | tf_op jit(solution)/shard_map/front/pallas_call | solution.py:756
  150.2 0.7 constant_dynamic-slice_fusion
  151.0 0.9 reshape.138
  151.8 0.1 dynamic-slice_bitcast_fusion
  151.9 0.3 copy.69
  152.2 1.8 copy.72
  154.0 0.6 broadcast_in_dim.15
  154.6 0.5 reshape.139
  155.1 0.6 copy-done.4
  155.7 0.1 multiply_reduce_fusion
  155.8 0.0 copy-start.3
  155.8 0.8 copy-done.2
  156.6 3.9 fusion.8
  160.6 0.2 multiply_reduce_fusion.1
  160.8 0.7 fusion.3.refs_0_
  161.5 88.6 %feed.1 = (f32[2,1,16,1536]{3,2,1,0:T(8,128)}, f32[2,1,16,1536]{3,2,1,0:T(8,128)}, bf16[4,4,32,384]{3,2,1,0:T(8,128)(2,1)}, f32[4,16,32]{2,1,0:T(8,128)}, bf16[2...) custom-call(bf16[2,1,16,1536]{3,2,1,0:T(8,128)(2,1)} %fusion.3.refs_, ...), custom_call_target="tpu_custom_call" | custom-call | tf_op jit(solution)/shard_map/feed/pallas_call | solution.py:931
  250.1 0.9 reshape.145
  251.0 0.1 stack_reshape.3
  251.1 0.6 pad_maximum_fusion.1.refs_7_
  251.8 146.7 %attend_back.1 = (bf16[2,2,4,4,2,2,96,384]{7,6,5,4,3,2,1,0:T(8,128)(2,1)}, f32[2,512,1536]{2,1,0:T(8,128)}, f32[4,2,96,384]{3,2,1,0:T(8,128)}, bf16[2,192,1536]{...) custom-call(bf16[2,528,1536]{2,1,0:T(8,128)(2,1)} %get-tuple-element.91.refs_0_, ...), custom_call_target="tpu_custom_call" | custom-call | tf_op jit(solution)/shard_map/attend_back/pallas_call | solution.py:1322
  398.5 16.2 %refresh.1 = (f32[1,1]{1,0:T(1,128)}, f32[2,512,1536]{2,1,0:T(8,128)}, f32[3,192,384]{2,1,0:T(8,128)}, f32[3,192,384]{2,1,0:T(8,128)}, f32[3,192,384]{2,1,0:T(8,...) custom-call(f32[8,128]{1,0:T(8,128)} %get-tuple-element.103.refs_0_,, ...), custom_call_target="tpu_custom_call" | custom-call | tf_op jit(solution)/shard_map/refresh/pallas_call | solution.py:1471
  414.7 0.7 copy.82
  415.4 0.7 copy.83
  (21 shorter events, 0.1 us)
Async XLA Ops:
  3.5 2.0 copy-start
  154.6 1.1 copy-start.4
  155.7 0.9 copy-start.2
  155.8 4.7 %copy-start.3 = (f32[4,2,16,384]{3,2,1,0:T(8,128)}, f32[4,2,16,384]{3,2,1,0:T(8,128)S(1)}, u32[]{:S(2)}) copy-start(f32[4,2,16,384]{3,2,1,0:T(8,128)S(1)} %multiply_reduce_fusion) | copy-start | bytes 589828
  156.6 4.1 copy-start.7
  156.6 4.1 copy-start.8
  160.6 1.0 copy-start.1
  398.5 16.2 %copy-start.5 = (f32[2,16,1536]{2,1,0:T(8,128)S(1)}, f32[2,16,1536]{2,1,0:T(8,128)}, u32[]{:S(2)}) copy-start(f32[2,16,1536]{2,1,0:T(8,128)} %get-tuple-element.176) | copy-start | bytes 589828
  398.5 16.9 %copy-start.6 = (f32[2,16,1536]{2,1,0:T(8,128)S(1)}, f32[2,16,1536]{2,1,0:T(8,128)}, u32[]{:S(2)}) copy-start(f32[2,16,1536]{2,1,0:T(8,128)} %get-tuple-element.177) | copy-start | bytes 589828

commit v4 on v3

--- a/solution.py
+++ b/solution.py
@@ -1534,12 +1534,10 @@
         return rows.reshape(t, 1, own_rows // t, width)
 
     weight_halves = halves(rows_d)
-    def as_pieces(wide):
-        return wide.reshape(rows_d, dp_count, units).transpose(1, 0, 2)
-
     ffn_pieces = jnp.concatenate(
-        [as_pieces(up_master.astype(half)), as_pieces(down_master.T.astype(half))], axis=2
-    )
+        [wide.reshape(rows_d, dp_count, units) for wide in (up_master, down_master.T)], axis=2
+    )
+    ffn_pieces = ffn_pieces.transpose(1, 0, 2).astype(half)
     slot_ids = mp_rank * slots + jnp.arange(slots)
     frame_ids = slot_ids // PATCHES
     keep = jnp.concatenate(

time: 417 us -> 417 us (level)
  no operation moved by 1% of the time
where the time goes in v4:
time: 417 us; the launch traced here: 416 us
  Pallas kernels  394 us (94%)
  local copies, waits for them, and re-layouts  12.7 us (3%)
  other arithmetic  5.27 us (1%)
    pallas_call x1, Pallas kernels, attend_back(): pl.pallas_call(functools.partial(attend_back_kernel, place, heads, scale,...  147 us
    pallas_call x1, Pallas kernels, front(): pl.pallas_call(functools.partial(front_kernel, place, heads, scale, halve...  142 us
    pallas_call x1, Pallas kernels, feed(): pl.pallas_call(functools.partial(feed_kernel, place, parts), in_specs=[hb...  88.6 us
    pallas_call x1, Pallas kernels, refresh(): pl.pallas_call(refresh_kernel, in_specs=[whole] * 4 + [hbm] + [whole] * l...  16.2 us

profile of v4, /device:TPU:0, one launch (start us, length us, event | category | flops | bytes accessed | tf_op | source)
XLA Modules:
  0.0 416.4 jit_solution(12691113117491707433)
XLA Ops:
  0.7 0.7 broadcast_compare_fusion
  1.4 0.6 reshape.149.refs_6_
  2.0 1.5 slice_reduce_fusion.1
  3.5 1.3 convert.9
  4.9 0.6 reshape.138
  5.5 0.2 copy.67
  5.7 0.5 copy-done
  6.2 0.6 reshape.139
  6.8 0.2 copy.68
  7.0 1.5 maximum_bitcast_fusion.refs_4_
  8.5 142.1 %front.1 = (bf16[2,2,4,4,2,2,96,384]{7,6,5,4,3,2,1,0:T(8,128)(2,1)}, bf16[2,2,2,4,2,1,16,1536]{7,6,5,4,3,2,1,0:T(8,128)(2,1)}, bf16[2,528,1536]{2,1,0:T(8,128)(2...) custom-call(f32[3,192,384]{2,1,0:T(8,128)} %refs_5_.3, ...), custom_call_target="tpu_custom_call" | custom-call | tf_op jit(solution)/shard_map/front/pallas_call | solution.py:756
  150.6 0.7 constant_dynamic-slice_fusion
  151.3 0.9 reshape.140
  152.2 0.1 dynamic-slice_bitcast_fusion
  152.3 0.3 copy.69
  152.5 1.8 copy.72
  154.3 0.6 broadcast_in_dim.15
  154.9 0.5 reshape.141
  155.5 0.6 copy-done.4
  156.1 0.1 multiply_reduce_fusion
  156.2 0.8 copy-done.2
  157.0 3.9 fusion.8
  160.9 0.2 multiply_reduce_fusion.1
  161.1 0.7 fusion.3.refs_0_
  161.9 88.6 %feed.1 = (f32[2,1,16,1536]{3,2,1,0:T(8,128)}, f32[2,1,16,1536]{3,2,1,0:T(8,128)}, bf16[4,4,32,384]{3,2,1,0:T(8,128)(2,1)}, f32[4,16,32]{2,1,0:T(8,128)}, bf16[2...) custom-call(bf16[2,1,16,1536]{3,2,1,0:T(8,128)(2,1)} %fusion.3.refs_, ...), custom_call_target="tpu_custom_call" | custom-call | tf_op jit(solution)/shard_map/feed/pallas_call | solution.py:931
  250.5 0.9 reshape.147
  251.4 0.1 stack_reshape.3
  251.5 0.6 pad_maximum_fusion.refs_7_
  252.1 146.7 %attend_back.1 = (bf16[2,2,4,4,2,2,96,384]{7,6,5,4,3,2,1,0:T(8,128)(2,1)}, f32[2,512,1536]{2,1,0:T(8,128)}, f32[4,2,96,384]{3,2,1,0:T(8,128)}, bf16[2,192,1536]{...) custom-call(bf16[2,528,1536]{2,1,0:T(8,128)(2,1)} %get-tuple-element.91.refs_0_, ...), custom_call_target="tpu_custom_call" | custom-call | tf_op jit(solution)/shard_map/attend_back/pallas_call | solution.py:1322
  398.9 16.2 %refresh.1 = (f32[1,1]{1,0:T(1,128)}, f32[2,512,1536]{2,1,0:T(8,128)}, f32[3,192,384]{2,1,0:T(8,128)}, f32[3,192,384]{2,1,0:T(8,128)}, f32[3,192,384]{2,1,0:T(8,...) custom-call(f32[8,128]{1,0:T(8,128)} %get-tuple-element.103.refs_0_,, ...), custom_call_target="tpu_custom_call" | custom-call | tf_op jit(solution)/shard_map/refresh/pallas_call | solution.py:1471
  415.0 0.7 copy.80
  415.7 0.7 copy.81
  (22 shorter events, 0.2 us)
Async XLA Ops:
  4.9 1.3 copy-start
  154.9 1.1 copy-start.4
  156.1 0.9 copy-start.2
  156.2 4.7 %copy-start.3 = (f32[4,2,16,384]{3,2,1,0:T(8,128)}, f32[4,2,16,384]{3,2,1,0:T(8,128)S(1)}, u32[]{:S(2)}) copy-start(f32[4,2,16,384]{3,2,1,0:T(8,128)S(1)} %multiply_reduce_fusion) | copy-start | bytes 589828
  157.0 4.1 copy-start.7
  157.0 4.1 copy-start.8
  160.9 1.0 copy-start.1
  398.8 16.2 %copy-start.5 = (f32[2,16,1536]{2,1,0:T(8,128)S(1)}, f32[2,16,1536]{2,1,0:T(8,128)}, u32[]{:S(2)}) copy-start(f32[2,16,1536]{2,1,0:T(8,128)} %get-tuple-element.174) | copy-start | bytes 589828
  398.8 16.9 %copy-start.6 = (f32[2,16,1536]{2,1,0:T(8,128)S(1)}, f32[2,16,1536]{2,1,0:T(8,128)}, u32[]{:S(2)}) copy-start(f32[2,16,1536]{2,1,0:T(8,128)} %get-tuple-element.175) | copy-start | bytes 589828
